TPU v7x, 128 devices: a whole 4x4x4 slice. The times are simulated.
128 devices in a mesh: wide: 64 (over x, z, y_lo, core), narrow: 2 (over y_hi).
Axes of the slice: x: 4, y: 4 (y_hi: 2, y_lo: 2; y = y_hi * 2 + y_lo), z: 4, core: 2. Of those that a mesh axis runs over, the one named last changes fastest.
Arguments:
- dosage: bfloat16 [2048, 131072], P(None, 'wide'), may hold values from -4 to 6, as said below
- annotations: int32 [128, 131072], P(None, 'wide'), may hold values from 0 to 1, as said below
- test_statistic_table: float32 [131072, 512], P('wide', 'narrow'), may hold values from 0 to 200
Outputs:
- ld_scores: float32 [128, 131072], P(None, ('wide', 'narrow'))
- fitted: float32 [131072, 512], P('wide', 'narrow')
Inputs may be any that keep to these rules, and one draw needn't show every extreme that they name: `dosage`: dosages of each variant follow a correlated process along the variants. `annotations`: 1 where a variant belongs to an annotation.
All inputs are finite; a program needn't handle non-finite values.
Results may differ from a plain program's by a relative error of at most 0.0023.
Values may be sent and summed in bfloat16 or wider, within the bound.
A program may use at most 128 MiB of HBM per device.

v0:
```python
import jax
import jax.numpy as jnp
from jax import lax
from jax.sharding import PartitionSpec as P

HALF = 1024


highest_precision = lax.Precision.HIGHEST


def extended_2(cells, sides, width):
    for axis, dim in sides:
        count = lax.axis_size(axis)
        ends = count - 1
        head = lax.slice_in_dim(cells, 0, width, axis=dim)
        tail = lax.slice_in_dim(cells, cells.shape[dim] - width, cells.shape[dim], axis=dim)
        cells = jnp.concatenate(
            [
                lax.ppermute(tail, axis, [(i, (i + 1) % count) for i in range(ends)]),
                cells,
                lax.ppermute(head, axis, [((i + 1) % count, i) for i in range(ends)]),
            ],
            axis=dim,
        )
    return cells


def band_weights(col_geno, row_geno, col_start, row_start, total_variants):
    products = lax.dot_general(
        col_geno, row_geno, (((0,), (0,)), ((), ())), preferred_element_type=jnp.float32
    )
    samples = row_geno.shape[0]
    correlation = products / samples
    squared = correlation * correlation
    adjusted = squared - (1.0 - squared) / (samples - 2)
    col_index = col_start + jnp.arange(col_geno.shape[1], dtype=jnp.int32)[:, None]
    row_index = row_start + jnp.arange(row_geno.shape[1], dtype=jnp.int32)[None, :]
    inside = (
        (jnp.abs(row_index - col_index) <= HALF) & (col_index >= 0) & (col_index < total_variants)
    )
    return jnp.where(inside, adjusted, 0.0).astype(jnp.bfloat16)


def shards(dosage, annotations, test_statistic_table):
    samples = dosage.shape[0]
    strip_cols = dosage.shape[1]
    half_width = strip_cols // 2
    total_variants = lax.axis_size("wide") * strip_cols
    wide_index = lax.axis_index("wide")
    narrow_index = lax.axis_index("narrow")
    values = dosage.astype(jnp.float32)
    average = jnp.mean(values, axis=0)
    centred_values = values - average[None, :]
    variance = jnp.mean(centred_values * centred_values, axis=0)
    standard = (centred_values / jnp.sqrt(variance + 1e-05)[None, :]).astype(jnp.bfloat16)
    counts = lax.psum(jnp.sum(annotations.astype(jnp.float32), axis=1), "wide")
    shares = counts / total_variants
    centred = (annotations.astype(jnp.float32) - shares[:, None]).astype(jnp.bfloat16)
    stacked = jnp.concatenate([standard, centred], axis=0)
    row_local = narrow_index * half_width
    strip_start = wide_index * strip_cols
    row_start = strip_start + row_local
    own_rows = lax.dynamic_slice_in_dim(standard, row_local, half_width, 1)
    extended = extended_2(stacked, (("wide", 1),), half_width)
    scores = jnp.zeros((centred.shape[0], half_width), jnp.float32)
    for offset in range(3):
        col_block = lax.dynamic_slice_in_dim(
            extended, row_local + offset * half_width, half_width, 1
        )
        weights = band_weights(
            col_block[:samples],
            own_rows,
            row_start - half_width + offset * half_width,
            row_start,
            total_variants,
        )
        scores = scores + jnp.dot(col_block[samples:], weights, preferred_element_type=jnp.float32)
    strip_scores = lax.all_gather(scores, "narrow", axis=1, tiled=True)
    chi_local = jnp.sum(test_statistic_table, axis=0)
    totals = lax.psum(jnp.sum(strip_scores, axis=1), "wide")
    score_mean = totals / total_variants
    deviation = strip_scores - score_mean[:, None]
    cross_local = lax.dot_general(
        deviation,
        deviation,
        (((1,), (1,)), ((), ())),
        precision=highest_precision,
        preferred_element_type=jnp.float32,
    )
    proj_local = jnp.dot(
        deviation,
        test_statistic_table,
        precision=highest_precision,
        preferred_element_type=jnp.float32,
    )
    cross_sum, proj_sum, dev_sum, chi_sum = lax.psum(
        (cross_local, proj_local, jnp.sum(deviation, axis=1), chi_local), "wide"
    )
    chi_mean = chi_sum / total_variants
    covariance = cross_sum / total_variants
    centred_proj = (
        proj_sum / total_variants - (dev_sum / total_variants)[:, None] * chi_mean[None, :]
    )
    spread = jnp.sqrt(jnp.diagonal(covariance) + 1e-05)
    gram_matrix = covariance / (spread[:, None] * spread[None, :])
    projection = centred_proj / spread[:, None]
    factor = jnp.linalg.cholesky(gram_matrix)
    coefficient = jax.scipy.linalg.cho_solve((factor, True), projection)
    standard_scores = (strip_scores - score_mean[:, None]) / spread[:, None]
    fitted = chi_mean[None, :] + lax.dot_general(
        standard_scores,
        coefficient,
        (((0,), (0,)), ((), ())),
        precision=highest_precision,
        preferred_element_type=jnp.float32,
    )
    own_scores = lax.dynamic_slice_in_dim(standard_scores, row_local, half_width, 1)
    return (own_scores, fitted)


def solution(mesh):
    in_specs = (P(None, "wide"), P(None, "wide"), P("wide", "narrow"))
    out_specs = (P(None, ("wide", "narrow")), P("wide", "narrow"))
    return jax.shard_map(shards, mesh=mesh, in_specs=in_specs, out_specs=out_specs, check_vma=False)
```

profile of v0, /device:TPU:1, one launch (start us, length us, event | category | flops | bytes accessed | tf_op | source)
XLA Modules:
  0.0 1174.4 jit_solution(18052722490963843743)
XLA Ops:
  7.2 4.9 convert_reduce_fusion
  13.0 2.2 fusion.2
  15.2 10.0 fusion.3
  25.4 140.8 %psum.42 = f32[128]{0:T(128)S(1)} all-reduce(f32[128]{0:T(128)S(1)} %convert_reduce_fusion.1), channel_id=1, replica_groups=mesh['wide'=64,'narrow'=2] {'wide'}, use_global_device_ids=true, to_apply=%region_3.0 | all-reduce | flops 128 | bytes 1024 | tf_op jit(solution)/shard_map/psum | solution.py:57
  166.4 12.3 %fusion.4 = (bf16[2176,1024]{1,0:T(8,128)(2,1)}, bf16[2176,1024]{1,0:T(8,128)(2,1)}) fusion(bf16[2048,2048]{1,0:T(8,128)(2,1)} %fusion.3, bf16[128,2048]{1,0:T(8,128)(2,1)S(1)} %subtract_convert_fusion), kind=kLoop, calls=%fused_computation.10 | loop fusion | flops 17825792 | bytes 17825792 | tf_op jit(solution)/shard_map/concatenate | solution.py:60
  178.7 7.8 collective-permute-start.1
  186.5 2.1 collective-permute-start
  188.7 89.7 %collective-permute-done.1 = bf16[2176,1024]{1,0:T(8,128)(2,1)} collective-permute-done((bf16[2176,1024]{1,0:T(8,128)(2,1)}, bf16[2176,1024]{1,0:T(8,128)(2,1)}, u32[]{:S(2)}, u32[]{:S(2)}) %collective-permute-start.1) | collective-permute-done | bytes 4456480 | tf_op jit(solution)/shard_map/ppermute | solution.py:22
  278.4 23.0 %pad_maximum_fusion = bf16[2176,4096]{1,0:T(8,128)(2,1)} fusion(bf16[2176,1024]{1,0:T(8,128)(2,1)} %collective-permute-done.1, bf16[128,2048]{1,0:T(8,128)(2,1)S(1)} %subtract_convert_fusion, bf16[2048,2048]{1,0:T(8,128)(2,1)} %fusion.3, bf16[2176,1024]{1,0:T(8,128)(2,1)} %collective-permute-done), kind=kLoop, calls=%fused_computation.5 | loop fusion | flops 71303168 | bytes 35651584 | tf_op jit(solution)/shard_map/concatenate | solution.py:18
  301.5 10.2 fusion.39
  311.6 11.2 fusion.44
  322.8 11.1 fusion.52
  334.0 23.5 %all-gather.2.cloned.1.call-done = f32[128,2048]{1,0:T(8,128)} async-done(((f32[128,1024]{1,0:T(8,128)}), f32[128,2048]{1,0:T(8,128)}) %all-gather.2.cloned.1.call-update) | async-done | bytes 1048592 | tf_op jit(solution)/shard_map/all_gather | solution.py:79
  357.5 1.4 reduce_sum.57
  358.9 138.5 %psum.43 = f32[128]{0:T(128)S(1)} all-reduce(f32[128]{0:T(128)S(1)} %reduce_sum.57), channel_id=1, replica_groups=mesh['wide'=64,'narrow'=2] {'wide'}, use_global_device_ids=true, to_apply=%region_5.6 | all-reduce | flops 128 | bytes 1024 | tf_op jit(solution)/shard_map/psum | solution.py:81
  497.4 3.3 fusion.59
  500.7 3.1 fusion.57
  504.1 489.7 %all-reduce.4.cloned.1.call-done = (f32[128,128]{0,1:T(8,128)}, f32[128,256]{1,0:T(8,128)}) async-done(((f32[128,128]{0,1:T(8,128)}, f32[128,256]{1,0:T(8,128)}), (f32[128,128]{0,1:T(8,128)}, f32[128,256]{1,0:T(8,128)})) %all-reduce.4.cloned.1.call-update) | async-done | bytes 196624 | tf_op jit(solution)/shard_map/psum | solution.py:97
  994.7 1.3 gather_fusion
  998.1 0.9 fusion.75
  999.1 11.7 cholesky.16
  1012.1 9.8 custom-call.10
  1021.9 141.4 %all-reduce = (f32[256]{0:T(256)S(1)}, f32[128]{0:T(128)S(1)}) all-reduce(f32[256]{0:T(256)S(1)} %reduce_sum.58, f32[128]{0:T(128)S(1)} %get-tuple-element.8), channel_id=1, replica_groups=mesh['wide'=64,'narrow'=2] {'wide'}, use_global_device_ids=true, to_apply=%region_8.9 | all-reduce | flops 384 | bytes 3072 | tf_op jit(solution)/shard_map/psum | solution.py:97
  1164.0 3.2 convolution_add_fusion
  (41 shorter events, 6.6 us)
Async XLA Ops:
  7.2 350.3 %all-gather.2.cloned.1.call-start = ((), (), s32[]{:S(2)}) async-start(), calls=%async_computation | async-start | bytes 1572864 | tf_op jit(solution)/shard_map/all_gather | solution.py:79
  7.2 5.8 copy-start
  15.2 10.0 copy-start.3
  178.7 99.7 %collective-permute-start.1 = (bf16[2176,1024]{1,0:T(8,128)(2,1)}, bf16[2176,1024]{1,0:T(8,128)(2,1)}, u32[]{:S(2)}, u32[]{:S(2)}) collective-permute-start(bf16[2176,1024]{1,0:T(8,128)(2,1)} %get-tuple-element.7), channel_id=1, source_target_pairs={{2,0},{4,2},{6,4},{8,6},{10,8},{12,10},{14,12},{16,14},{18,16},{20... | collective-permute-start | bytes 13369352 | tf_op jit(solution)/shard_map/ppermute | solution.py:22
  186.5 91.9 %collective-permute-start = (bf16[2176,1024]{1,0:T(8,128)(2,1)}, bf16[2176,1024]{1,0:T(8,128)(2,1)}, u32[]{:S(2)}, u32[]{:S(2)}) collective-permute-start(bf16[2176,1024]{1,0:T(8,128)(2,1)} %get-tuple-element.6), channel_id=1, source_target_pairs={{0,2},{2,4},{4,6},{6,8},{8,10},{10,12},{12,14},{14,16},{16,18},{18... | collective-permute-start | bytes 13369352 | tf_op jit(solution)/shard_map/ppermute | solution.py:20
  322.8 177.9 %copy-start.2 = (f32[2048,256]{1,0:T(8,128)S(1)}, f32[2048,256]{1,0:T(8,128)}, u32[]{:S(2)}) copy-start(f32[2048,256]{1,0:T(8,128)} %param.5) | copy-start | bytes 6291460
  334.0 659.8 %all-reduce.4.cloned.1.call-start = ((), (), s32[]{:S(2)}) async-start(), calls=%async_computation.1 | async-start | bytes 393216 | tf_op jit(solution)/shard_map/psum | solution.py:97
  357.5 639.4 %copy-start.1 = (f32[128,2048]{1,0:T(8,128)S(1)}, f32[128,2048]{1,0:T(8,128)}, u32[]{:S(2)}) copy-start(f32[128,2048]{1,0:T(8,128)} %all-gather.2.cloned.1.call-done) | copy-start | bytes 3145732
  993.8 169.6 %copy-start.4 = (f32[128,256]{1,0:T(8,128)S(1)}, f32[128,256]{1,0:T(8,128)}, u32[]{:S(2)}) copy-start(f32[128,256]{1,0:T(8,128)} %get-tuple-element.5) | copy-start | bytes 393220
Sparse Core Ops, SparseCore 0:
  334.1 23.3 all-gather.1
  503.9 489.8 all-reduce.3
where the time goes:
time: 1180 us; the launch traced here: 1170 us
  waiting for transfers between devices  603 us (51%)
  blocking collectives  421 us (36%)
  other arithmetic  80.5 us (7%)
  matrix products  42.6 us (4%)
  between operations  14.6 us (1%)
    psum x1, waiting for transfers between devices, shards(): lax.psum((cross_local, proj_local, jnp.sum(deviation, axis=1), chi_local)...  490 us
    psum x1, blocking collectives, shards(): lax.psum((cross_local, proj_local, jnp.sum(deviation, axis=1), chi_local)...  141 us
    psum x1, blocking collectives, shards(): counts = lax.psum(jnp.sum(annotations.astype(jnp.float32), axis=1), 'wide')  141 us
    psum x1, blocking collectives, shards(): totals = lax.psum(jnp.sum(strip_scores, axis=1), 'wide')  138 us
    ppermute x1, waiting for transfers between devices, extended_2(): lax.ppermute(head, axis, [((i + 1) % count, i) for i in range(ends)])  89.7 us
    dot_general x3, matrix products, shards(): jnp.dot(col_block[samples:], weights, preferred_element_type=jnp.float32)  32.5 us
  transfers between devices with their start and end apart: 4, of which 3 were waited for; matrix products, arithmetic and copies ran while one was open for 0% of the time, Pallas kernels for 0%

commit v1 on v0

--- a/solution.py
+++ b/solution.py
@@ -1,12 +1,14 @@
+import functools
+
 import jax
 import jax.numpy as jnp
 from jax import lax
+from jax.experimental import pallas as pl
+from jax.experimental.pallas import tpu as pltpu
 from jax.sharding import PartitionSpec as P
 
 HALF = 1024
-
-
-highest_precision = lax.Precision.HIGHEST
+MESH = pl.DeviceIdType.MESH
 
 
 def extended_2(cells, sides, width):
@@ -40,6 +42,220 @@
         (jnp.abs(row_index - col_index) <= HALF) & (col_index >= 0) & (col_index < total_variants)
     )
     return jnp.where(inside, adjusted, 0.0).astype(jnp.bfloat16)
+
+
+def split(x):
+    hi = x.astype(jnp.bfloat16)
+    return hi, (x - hi.astype(jnp.float32)).astype(jnp.bfloat16)
+
+
+def dot3(a, b, dims):
+    ah, al = a
+    bh, bl = b
+    dg = functools.partial(
+        lax.dot_general, dimension_numbers=(dims, ((), ())), preferred_element_type=jnp.float32
+    )
+    return dg(ah, bh) + (dg(ah, bl) + dg(al, bh))
+
+
+TILES = 64
+
+
+def stats_kernel(s_ref, t_ref, out_ref, part, got1, sum1, got2, sum2, got3, send, recv):
+    w = lax.axis_index("wide")
+    g = lax.rem(w, 8)
+    h = lax.div(w, 8)
+
+    barrier = pltpu.get_barrier_semaphore()
+    for d in range(1, 8):
+        pl.semaphore_signal(
+            barrier, inc=1, device_id={"wide": w - g + lax.rem(g + d, 8)}, device_id_type=MESH
+        )
+        pl.semaphore_signal(
+            barrier, inc=1, device_id={"wide": lax.rem(h + d, 8) * 8 + g}, device_id_type=MESH
+        )
+
+    s = s_ref[...]
+    t = t_ref[...]
+    ss = split(s)
+    ts = split(t)
+    part[0:128, :] = dot3(ss, ss, ((1,), (1,)))
+    proj = dot3(ss, ts, ((1,), (0,)))
+    part[128:256, :] = proj[:, :128]
+    part[256:384, :] = proj[:, 128:]
+    ones = jnp.ones((8, s.shape[1]), jnp.bfloat16)
+    dg = functools.partial(lax.dot_general, preferred_element_type=jnp.float32)
+    ssum = dg(ones, ss[0], (((1,), (1,)), ((), ()))) + dg(ones, ss[1], (((1,), (1,)), ((), ())))
+    tsum = jnp.sum(t, axis=0, keepdims=True)
+    rows = lax.broadcasted_iota(jnp.int32, (8, 128), 0)
+    sums = jnp.where(rows == 0, ssum, 0.0)
+    sums = jnp.where(rows == 1, tsum[:, :128], sums)
+    sums = jnp.where(rows == 2, tsum[:, 128:], sums)
+    part[384:392, :] = sums
+    part[392:512, :] = jnp.zeros((120, 128), jnp.float32)
+
+    pl.semaphore_wait(barrier, 14)
+
+    def in_block(d):
+        return lax.rem(g + d, 8)
+
+    def across(d):
+        return lax.rem(h + d, 8)
+
+    def copy1(d):
+        p = in_block(d)
+        return pltpu.make_async_remote_copy(
+            src_ref=part.at[pl.ds(pl.multiple_of(p * 64, 64), 64)],
+            dst_ref=got1.at[d - 1],
+            send_sem=send.at[0, d],
+            recv_sem=recv.at[0, d],
+            device_id={"wide": w - g + p},
+            device_id_type=MESH,
+        )
+
+    def copy2(d):
+        p = across(d)
+        return pltpu.make_async_remote_copy(
+            src_ref=sum1.at[pl.ds(pl.multiple_of(p * 8, 8), 8)],
+            dst_ref=got2.at[d - 1],
+            send_sem=send.at[1, d],
+            recv_sem=recv.at[1, d],
+            device_id={"wide": p * 8 + g},
+            device_id_type=MESH,
+        )
+
+    def copy3(d):
+        return pltpu.make_async_remote_copy(
+            src_ref=sum2,
+            dst_ref=got3.at[pl.ds(pl.multiple_of(h * 8, 8), 8)],
+            send_sem=send.at[2, d],
+            recv_sem=recv.at[2, d],
+            device_id={"wide": across(d) * 8 + g},
+            device_id_type=MESH,
+        )
+
+    def copy4(d):
+        return pltpu.make_async_remote_copy(
+            src_ref=got3,
+            dst_ref=out_ref.at[pl.ds(pl.multiple_of(g * 64, 64), 64)],
+            send_sem=send.at[3, d],
+            recv_sem=recv.at[3, d],
+            device_id={"wide": w - g + in_block(d)},
+            device_id_type=MESH,
+        )
+
+    for d in range(1, 8):
+        copy1(d).start()
+    acc = part[pl.ds(pl.multiple_of(g * 64, 64), 64), :]
+    for d in range(1, 8):
+        copy1(d).wait_recv()
+        acc = acc + got1[d - 1]
+    sum1[...] = acc
+    for d in range(1, 8):
+        copy2(d).start()
+    acc = sum1[pl.ds(pl.multiple_of(h * 8, 8), 8), :]
+    for d in range(1, 8):
+        copy2(d).wait_recv()
+        acc = acc + got2[d - 1]
+    sum2[...] = acc
+    for d in range(1, 8):
+        copy3(d).start()
+    got3[pl.ds(pl.multiple_of(h * 8, 8), 8), :] = acc
+    for d in range(1, 8):
+        copy3(d).wait_recv()
+    for d in range(1, 8):
+        copy4(d).start()
+    out_ref[pl.ds(pl.multiple_of(g * 64, 64), 64), :] = got3[...]
+    for d in range(1, 8):
+        copy4(d).wait_recv()
+    for copy in (copy1, copy2, copy3, copy4):
+        for d in range(1, 8):
+            copy(d).wait_send()
+
+
+def stats(scores, table):
+    f32 = jnp.float32
+    return pl.pallas_call(
+        stats_kernel,
+        out_shape=jax.ShapeDtypeStruct((TILES * 8, 128), f32),
+        in_specs=[pl.BlockSpec(memory_space=pltpu.VMEM)] * 2,
+        out_specs=pl.BlockSpec(memory_space=pltpu.VMEM),
+        scratch_shapes=[
+            pltpu.VMEM((TILES * 8, 128), f32),
+            pltpu.VMEM((7, 64, 128), f32),
+            pltpu.VMEM((64, 128), f32),
+            pltpu.VMEM((7, 8, 128), f32),
+            pltpu.VMEM((8, 128), f32),
+            pltpu.VMEM((64, 128), f32),
+            pltpu.SemaphoreType.DMA((4, 8)),
+            pltpu.SemaphoreType.DMA((4, 8)),
+        ],
+        compiler_params=pltpu.CompilerParams(
+            collective_id=1, has_side_effects=True, vmem_limit_bytes=32 * 1024 * 1024
+        ),
+        name="stats",
+    )(scores, table)
+
+
+def finish_kernel(total_variants, p_ref, s_ref, ld_ref, fit_ref):
+    n = lax.axis_index("narrow")
+    scale = 1.0 / total_variants
+    sums = p_ref[384:392, :] * scale
+    m_row = sums[0:1, :]
+    chi = jnp.concatenate([sums[1:2, :], sums[2:3, :]], axis=1)
+    ri = lax.broadcasted_iota(jnp.int32, (128, 128), 0)
+    ci = lax.broadcasted_iota(jnp.int32, (128, 128), 1)
+    eye = ri == ci
+    m_col = jnp.sum(jnp.where(eye, jnp.broadcast_to(m_row, (128, 128)), 0.0), axis=1, keepdims=True)
+    cov = p_ref[0:128, :] * scale - m_col * m_row
+    proj = jnp.concatenate([p_ref[128:256, :], p_ref[256:384, :]], axis=1) * scale - m_col * chi
+    var = jnp.sum(jnp.where(eye, cov, 0.0), axis=1, keepdims=True)
+    rstd = 1.0 / jnp.sqrt(var + 1e-05)
+
+    half = ld_ref.shape[1]
+    own = s_ref[:, pl.ds(pl.multiple_of(n * half, half), half)]
+    ld_ref[...] = (own - m_col) * rstd
+
+    sub = lax.broadcasted_iota(jnp.int32, (8, 1), 0)
+
+    def step(i, carry):
+        a, b = carry
+        for r in range(8):
+            col = a[:, r : r + 1]
+            ra = a[r : r + 1, :]
+            rb = b[r : r + 1, :]
+            inv = 1.0 / a[r : r + 1, r : r + 1]
+            ra = ra * inv
+            rb = rb * inv
+            a2 = a - col * ra
+            b2 = b - col * rb
+            here = sub == r
+            a = jnp.concatenate([jnp.where(here, ra, a2[:8]), a2[8:]], axis=0)
+            b = jnp.concatenate([jnp.where(here, rb, b2[:8]), b2[8:]], axis=0)
+        a = pltpu.roll(jnp.concatenate([a[8:], a[:8]], axis=0), 120, 1)
+        b = jnp.concatenate([b[8:], b[:8]], axis=0)
+        return a, b
+
+    _, coef = lax.fori_loop(0, 16, step, (cov, proj))
+    cs = split(coef)
+    rows = 256
+    for k in range(fit_ref.shape[0] // rows):
+        dev = (s_ref[:, k * rows : (k + 1) * rows] - m_col).T
+        fit_ref[k * rows : (k + 1) * rows, :] = chi + dot3(split(dev), cs, ((1,), (0,)))
+
+
+def finish(totals, scores, traits, total_variants):
+    return pl.pallas_call(
+        functools.partial(finish_kernel, total_variants),
+        out_shape=(
+            jax.ShapeDtypeStruct((128, scores.shape[1] // 2), jnp.float32),
+            jax.ShapeDtypeStruct((scores.shape[1], traits), jnp.float32),
+        ),
+        in_specs=[pl.BlockSpec(memory_space=pltpu.VMEM)] * 2,
+        out_specs=(pl.BlockSpec(memory_space=pltpu.VMEM),) * 2,
+        compiler_params=pltpu.CompilerParams(vmem_limit_bytes=32 * 1024 * 1024),
+        name="finish",
+    )(totals, scores)
 
 
 def shards(dosage, annotations, test_statistic_table):
@@ -77,46 +293,8 @@
         )
         scores = scores + jnp.dot(col_block[samples:], weights, preferred_element_type=jnp.float32)
     strip_scores = lax.all_gather(scores, "narrow", axis=1, tiled=True)
-    chi_local = jnp.sum(test_statistic_table, axis=0)
-    totals = lax.psum(jnp.sum(strip_scores, axis=1), "wide")
-    score_mean = totals / total_variants
-    deviation = strip_scores - score_mean[:, None]
-    cross_local = lax.dot_general(
-        deviation,
-        deviation,
-        (((1,), (1,)), ((), ())),
-        precision=highest_precision,
-        preferred_element_type=jnp.float32,
-    )
-    proj_local = jnp.dot(
-        deviation,
-        test_statistic_table,
-        precision=highest_precision,
-        preferred_element_type=jnp.float32,
-    )
-    cross_sum, proj_sum, dev_sum, chi_sum = lax.psum(
-        (cross_local, proj_local, jnp.sum(deviation, axis=1), chi_local), "wide"
-    )
-    chi_mean = chi_sum / total_variants
-    covariance = cross_sum / total_variants
-    centred_proj = (
-        proj_sum / total_variants - (dev_sum / total_variants)[:, None] * chi_mean[None, :]
-    )
-    spread = jnp.sqrt(jnp.diagonal(covariance) + 1e-05)
-    gram_matrix = covariance / (spread[:, None] * spread[None, :])
-    projection = centred_proj / spread[:, None]
-    factor = jnp.linalg.cholesky(gram_matrix)
-    coefficient = jax.scipy.linalg.cho_solve((factor, True), projection)
-    standard_scores = (strip_scores - score_mean[:, None]) / spread[:, None]
-    fitted = chi_mean[None, :] + lax.dot_general(
-        standard_scores,
-        coefficient,
-        (((0,), (0,)), ((), ())),
-        precision=highest_precision,
-        preferred_element_type=jnp.float32,
-    )
-    own_scores = lax.dynamic_slice_in_dim(standard_scores, row_local, half_width, 1)
-    return (own_scores, fitted)
+    totals = stats(strip_scores, test_statistic_table)
+    return finish(totals, strip_scores, test_statistic_table.shape[1], total_variants)
 
 
 def solution(mesh):

time: 1180 us -> 403 us (0.34)
  waiting for transfers between devices: 603 us -> 113 us
  blocking collectives: 421 us -> 141 us
  Pallas kernels: 0 us -> 38.3 us
  other arithmetic: 80.5 us -> 52.9 us
    psum x1 -> x0, waiting for transfers between devices: 490 us -> none  [shards(): lax.psum((cross_local, proj_local, jnp.sum(deviation, axis=1), chi_local)...]
    psum x2 -> x0, blocking collectives: 280 us -> none  [the longest x1 141 us: shards(): lax.psum((cross_local, proj_local, jnp.sum(deviation, axis=1), chi_local)...]
    pallas_call x0 -> x2, Pallas kernels: none -> 38.3 us  [the longest x1 23.5 us: stats(): pl.pallas_call(stats_kernel, out_shape=jax.ShapeDtypeStruct((TILES * 8, 1...]
    another operation x5 -> x0, other arithmetic: 22.9 us -> none  [the longest x3 12.4 us: shards(): factor = jnp.linalg.cholesky(gram_matrix)]
  transfers between devices with their start and end apart: 4 -> 3, of which waited for: 3 -> 2; matrix products, arithmetic and copies ran while one was open for 0% -> 0% of each run, Pallas kernels for 0% -> 0%
where the time goes in v1:
time: 403 us
  blocking collectives  141 us (35%)
  waiting for transfers between devices  113 us (28%)
  other arithmetic  52.9 us (13%)
  Pallas kernels  38.3 us (10%)
  matrix products  31.6 us (8%)
  between operations  14.1 us (3%)
  starting transfers between devices  9.96 us (2%)
    psum x1, blocking collectives, shards(): counts = lax.psum(jnp.sum(annotations.astype(jnp.float32), axis=1), 'wide')  141 us
    ppermute x1, waiting for transfers between devices, extended_2(): lax.ppermute(head, axis, [((i + 1) % count, i) for i in range(ends)])  89.7 us
    dot_general x3, matrix products, shards(): jnp.dot(col_block[samples:], weights, preferred_element_type=jnp.float32)  31.6 us
    all_gather x1, waiting for transfers between devices, shards(): strip_scores = lax.all_gather(scores, 'narrow', axis=1, tiled=True)  23.5 us
    pallas_call x1, Pallas kernels, stats(): pl.pallas_call(stats_kernel, out_shape=jax.ShapeDtypeStruct((TILES * 8, 1...  23.5 us
    concatenate x1, other arithmetic, extended_2(): jnp.concatenate([lax.ppermute(tail, axis, [(i, (i + 1) % count) for i in...  23 us
    pallas_call x1, Pallas kernels, finish(): pl.pallas_call(functools.partial(finish_kernel, total_variants), out_shap...  14.7 us
    concatenate x1, other arithmetic, shards(): stacked = jnp.concatenate([standard, centred], axis=0)  12.4 us
  transfers between devices with their start and end apart: 3, of which 2 were waited for; matrix products, arithmetic and copies ran while one was open for 0% of the time, Pallas kernels for 0%

profile of v1, /device:TPU:1, one launch (start us, length us, event | category | flops | bytes accessed | tf_op | source)
XLA Modules:
  0.0 403.0 jit_solution(11141852394127606577)
XLA Ops:
  7.2 0.0 all-gather.2.cloned.1.call-start
  7.2 0.0 copy-start.2
  7.2 4.9 %convert_reduce_fusion = f32[2048]{0:T(1024)S(1)} fusion(bf16[2048,2048]{1,0:T(8,128)(2,1)} %param.3), kind=kLoop, calls=%fused_computation.1 | loop fusion | flops 8386560 | bytes 8396800 | tf_op jit(solution)/shard_map/reduce_sum | solution.py:269
  12.2 0.8 copy-done.2
  13.0 2.2 fusion.2
  15.2 10.0 %fusion.3 = bf16[2048,2048]{1,0:T(8,128)(2,1)} fusion(bf16[2048,2048]{1,0:T(8,128)(2,1)} %param.3, f32[2048]{0:T(1024)S(1)} %add_sqrt_fusion, f32[2048]{0:T(1024)S(1)} %broadcast_multiply_fusion), kind=kLoop, calls=%fused_computation.6 | loop fusion | flops 16777216 | bytes 16793600 | tf_op jit(solution)/shard_map/convert_element_type | solution.py:272
  25.3 0.2 convert_reduce_fusion.1
  25.4 140.8 %psum.7 = f32[128]{0:T(128)S(1)} all-reduce(f32[128]{0:T(128)S(1)} %convert_reduce_fusion.1), channel_id=1, replica_groups=mesh['wide'=64,'narrow'=2] {'wide'}, use_global_device_ids=true, to_apply=%region_3.0 | all-reduce | flops 128 | bytes 1024 | tf_op jit(solution)/shard_map/psum | solution.py:273
  166.2 0.2 subtract_convert_fusion
  166.4 12.4 %fusion.4 = (bf16[2176,1024]{1,0:T(8,128)(2,1)}, bf16[2176,1024]{1,0:T(8,128)(2,1)}) fusion(bf16[2048,2048]{1,0:T(8,128)(2,1)} %fusion.3, bf16[128,2048]{1,0:T(8,128)(2,1)S(1)} %subtract_convert_fusion), kind=kLoop, calls=%fused_computation.9 | loop fusion | flops 17825792 | bytes 17825792 | tf_op jit(solution)/shard_map/concatenate | solution.py:276
  178.7 7.8 %collective-permute-start.1 = (bf16[2176,1024]{1,0:T(8,128)(2,1)}, bf16[2176,1024]{1,0:T(8,128)(2,1)}, u32[]{:S(2)}, u32[]{:S(2)}) collective-permute-start(bf16[2176,1024]{1,0:T(8,128)(2,1)} %get-tuple-element.3), channel_id=1, source_target_pairs={{2,0},{4,2},{6,4},{8,6},{10,8},{12,10},{14,12},{16,14},{18,16},{20... | collective-permute-start | bytes 13369352 | tf_op jit(solution)/shard_map/ppermute | solution.py:24
  186.6 2.1 collective-permute-start
  188.7 89.7 %collective-permute-done.1 = bf16[2176,1024]{1,0:T(8,128)(2,1)} collective-permute-done((bf16[2176,1024]{1,0:T(8,128)(2,1)}, bf16[2176,1024]{1,0:T(8,128)(2,1)}, u32[]{:S(2)}, u32[]{:S(2)}) %collective-permute-start.1) | collective-permute-done | bytes 4456480 | tf_op jit(solution)/shard_map/ppermute | solution.py:24
  278.4 0.0 collective-permute-done
  278.4 23.0 %pad_maximum_fusion = bf16[2176,4096]{1,0:T(8,128)(2,1)} fusion(bf16[2176,1024]{1,0:T(8,128)(2,1)} %collective-permute-done.1, bf16[128,2048]{1,0:T(8,128)(2,1)S(1)} %subtract_convert_fusion, bf16[2048,2048]{1,0:T(8,128)(2,1)} %fusion.3, bf16[2176,1024]{1,0:T(8,128)(2,1)} %collective-permute-done), kind=kLoop, calls=%fused_computation.4 | loop fusion | flops 71303168 | bytes 35651584 | tf_op jit(solution)/shard_map/concatenate | solution.py:20
  301.5 10.2 %fusion.39 = f32[128,1024]{1,0:T(8,128)S(1)} fusion(bf16[2048,2048]{1,0:T(8,128)(2,1)} %fusion.3, s32[]{:T(128)S(6)} %select_n.23, bf16[2176,4096]{1,0:T(8,128)(2,1)} %pad_maximum_fusion, s32[]{:T(128)S(6)} %select_n.25, s32[1024]{0:T(1024)S(1)} %get-tuple-element.11, pred[1024]{0:T(1024)(128)(4,1)S(1)} %get-tuple-element.4, ...), kind=kOutput, calls=%fused_computation.33 | convolution fusion | flops 4575985664 | bytes 9187328 | tf_op jit(solution)/shard_map/dot_general | solution.py:294
  311.6 10.4 %fusion.44 = f32[128,1024]{1,0:T(8,128)S(1)} fusion(bf16[2048,2048]{1,0:T(8,128)(2,1)} %fusion.3, s32[]{:T(128)S(6)} %select_n.23, bf16[2176,4096]{1,0:T(8,128)(2,1)} %pad_maximum_fusion, s32[]{:T(128)S(6)} %select_n.27, s32[1024]{0:T(1024)S(1)} %iota_add_fusion, s32[1024]{0:T(1024)S(1)} %get-tuple-element.11, pred[1024]{0:T(1024)(128)(4,1)S(1)} %get-tuple-element.6, ...), kind=kOutput, calls=%fused_computation.34 | convolution fusion | flops 4575985664 | bytes 9187328 | tf_op jit(solution)/shard_map/dot_general | solution.py:294
  322.0 0.0 copy-start.1
  322.0 11.1 %fusion.52 = f32[128,1024]{1,0:T(8,128)} fusion(f32[128,1024]{1,0:T(8,128)S(1)} %fusion.44, f32[128,1024]{1,0:T(8,128)S(1)} %fusion.39, bf16[2048,2048]{1,0:T(8,128)(2,1)} %fusion.3, s32[]{:T(128)S(6)} %select_n.23, bf16[2176,4096]{1,0:T(8,128)(2,1)} %pad_maximum_fusion, s32[]{:T(128)S(6)} %select_n.22, s32[1024]{0:T(1024)S(1)} %get-tuple-element.10, ...), kind=kOutput, calls=%fused_computation.36 | convolution fusion | flops 4576247808 | bytes 10235904 | tf_op jit(solution)/shard_map/dot_general | solution.py:294
  333.1 0.0 all-gather.2.cloned.1.call-update
  333.1 23.5 %all-gather.2.cloned.1.call-done.s_ref = f32[128,2048]{1,0:T(8,128)} async-done(((f32[128,1024]{1,0:T(8,128)}), f32[128,2048]{1,0:T(8,128)}) %all-gather.2.cloned.1.call-update) | async-done | bytes 1048592 | tf_op jit(solution)/shard_map/all_gather | solution.py:295
  356.7 1.2 copy-done
  357.9 23.5 %stats.1.p_ref = f32[512,128]{1,0:T(8,128)S(1)} custom-call(f32[128,2048]{1,0:T(8,128)S(1)} %copy-done, f32[2048,256]{1,0:T(8,128)S(1)} %copy-done.1), custom_call_target="tpu_custom_call" | custom-call | tf_op jit(solution)/shard_map/stats/pallas_call | solution.py:178
  381.5 14.7 %finish.1 = (f32[128,1024]{1,0:T(8,128)}, f32[2048,256]{1,0:T(8,128)}) custom-call(f32[512,128]{1,0:T(8,128)S(1)} %stats.1.p_ref, f32[128,2048]{1,0:T(8,128)S(1)} %copy-done), custom_call_target="tpu_custom_call" | custom-call | tf_op jit(solution)/shard_map/finish/pallas_call | solution.py:248
  (12 shorter events, 0.1 us)
Async XLA Ops:
  7.2 349.5 %all-gather.2.cloned.1.call-start = ((), (), s32[]{:S(2)}) async-start(), calls=%async_computation | async-start | bytes 1572864 | tf_op jit(solution)/shard_map/all_gather | solution.py:295
  7.2 5.8 %copy-start.2 = (bf16[2048,2048]{1,0:T(8,128)(2,1)S(1)}, bf16[2048,2048]{1,0:T(8,128)(2,1)}, u32[]{:S(2)}) copy-start(bf16[2048,2048]{1,0:T(8,128)(2,1)} %param.3) | copy-start | bytes 25165828
  15.2 10.0 %copy-start.3 = (s32[128,2048]{1,0:T(8,128)S(1)}, s32[128,2048]{1,0:T(8,128)}, u32[]{:S(2)}) copy-start(s32[128,2048]{1,0:T(8,128)} %param.4) | copy-start | bytes 3145732
  178.7 99.7 %collective-permute-start.1 = (bf16[2176,1024]{1,0:T(8,128)(2,1)}, bf16[2176,1024]{1,0:T(8,128)(2,1)}, u32[]{:S(2)}, u32[]{:S(2)}) collective-permute-start(bf16[2176,1024]{1,0:T(8,128)(2,1)} %get-tuple-element.3), channel_id=1, source_target_pairs={{2,0},{4,2},{6,4},{8,6},{10,8},{12,10},{14,12},{16,14},{18,16},{20... | collective-permute-start | bytes 13369352 | tf_op jit(solution)/shard_map/ppermute | solution.py:24
  186.6 91.9 %collective-permute-start = (bf16[2176,1024]{1,0:T(8,128)(2,1)}, bf16[2176,1024]{1,0:T(8,128)(2,1)}, u32[]{:S(2)}, u32[]{:S(2)}) collective-permute-start(bf16[2176,1024]{1,0:T(8,128)(2,1)} %get-tuple-element.2), channel_id=1, source_target_pairs={{0,2},{2,4},{4,6},{6,8},{8,10},{10,12},{12,14},{14,16},{16,18},{18... | collective-permute-start | bytes 13369352 | tf_op jit(solution)/shard_map/ppermute | solution.py:22
  322.0 34.7 %copy-start.1 = (f32[2048,256]{1,0:T(8,128)S(1)}, f32[2048,256]{1,0:T(8,128)}, u32[]{:S(2)}) copy-start(f32[2048,256]{1,0:T(8,128)} %t_ref.1) | copy-start | bytes 6291460
  356.7 1.2 copy-start
Sparse Core Ops, SparseCore 0:
  333.3 23.3 all-gather.1

commit v2 on v1

--- a/solution.py
+++ b/solution.py
@@ -7,41 +7,7 @@
 from jax.experimental.pallas import tpu as pltpu
 from jax.sharding import PartitionSpec as P
 
-HALF = 1024
 MESH = pl.DeviceIdType.MESH
-
-
-def extended_2(cells, sides, width):
-    for axis, dim in sides:
-        count = lax.axis_size(axis)
-        ends = count - 1
-        head = lax.slice_in_dim(cells, 0, width, axis=dim)
-        tail = lax.slice_in_dim(cells, cells.shape[dim] - width, cells.shape[dim], axis=dim)
-        cells = jnp.concatenate(
-            [
-                lax.ppermute(tail, axis, [(i, (i + 1) % count) for i in range(ends)]),
-                cells,
-                lax.ppermute(head, axis, [((i + 1) % count, i) for i in range(ends)]),
-            ],
-            axis=dim,
-        )
-    return cells
-
-
-def band_weights(col_geno, row_geno, col_start, row_start, total_variants):
-    products = lax.dot_general(
-        col_geno, row_geno, (((0,), (0,)), ((), ())), preferred_element_type=jnp.float32
-    )
-    samples = row_geno.shape[0]
-    correlation = products / samples
-    squared = correlation * correlation
-    adjusted = squared - (1.0 - squared) / (samples - 2)
-    col_index = col_start + jnp.arange(col_geno.shape[1], dtype=jnp.int32)[:, None]
-    row_index = row_start + jnp.arange(row_geno.shape[1], dtype=jnp.int32)[None, :]
-    inside = (
-        (jnp.abs(row_index - col_index) <= HALF) & (col_index >= 0) & (col_index < total_variants)
-    )
-    return jnp.where(inside, adjusted, 0.0).astype(jnp.bfloat16)
 
 
 def split(x):
@@ -56,6 +22,367 @@
         lax.dot_general, dimension_numbers=(dims, ((), ())), preferred_element_type=jnp.float32
     )
     return dg(ah, bh) + (dg(ah, bl) + dg(al, bh))
+
+
+CH = 256
+ROWS = 144
+FAR = 4096.0
+
+
+def scores_kernel(
+    total_variants, x_ref, ann_ref, out_ref,
+    geno, genot, annot, acc, wbuf, cnt, cnt_got, twin_out, twin_got, halo_out, halo_got,
+    load_sem, send, recv, csend, crecv,
+):
+    f32 = jnp.float32
+    bf16 = jnp.bfloat16
+    w = lax.axis_index("wide")
+    n = lax.axis_index("narrow")
+    wides = lax.axis_size("wide")
+    samples = x_ref.shape[0]
+    core = lax.rem(w, 2)
+    chip = lax.div(w, 2)
+    g = lax.rem(w, 8)
+    h = lax.div(w, 8)
+    groups = wides // 8
+    mate = w + 1 - 2 * core
+    over = lax.rem(w + 2 * core - 1 + wides, wides)
+    left_chip = lax.rem(chip + core - 1 + wides // 2, wides // 2)
+    turned = lax.rem(left_chip, 2)
+    p = n + turned - 2 * n * turned
+    ob = core * 4
+    mb = 4 - ob
+    csl = 2 * core + p
+
+    def device(wide, narrow):
+        return {"wide": wide, "narrow": narrow}
+
+    def chunk_of(t):
+        rest = ob + lax.rem(csl + t + 4, 4)
+        return jnp.where(t == 0, ob + csl, jnp.where(t <= 4, mb + t - 1, rest))
+
+    def load(t):
+        c = chunk_of(jnp.int32(t))
+        return pltpu.make_async_copy(
+            x_ref.at[:, pl.ds(pl.multiple_of(c * CH, CH), CH)], geno.at[c], load_sem.at[t]
+        )
+
+    for t in range(8):
+        load(t).start()
+
+    barrier = pltpu.get_barrier_semaphore()
+
+    def hello(wide, narrow):
+        pl.semaphore_signal(barrier, inc=1, device_id=device(wide, narrow), device_id_type=MESH)
+
+    for d in range(1, 8):
+        hello(w - g + lax.rem(g + d, 8), n)
+    for d in range(1, groups):
+        hello(lax.rem(h + d, groups) * 8 + g, n)
+    hello(w, 1 - n)
+    hello(over, 0)
+    hello(over, 1)
+
+    tail = jnp.where(lax.broadcasted_iota(jnp.int32, (16, CH), 0) == 0, 1.0, 0.0).astype(bf16)
+    count = jnp.zeros((8, 128), f32)
+    for c in range(8):
+        a = ann_ref[:, c * CH : (c + 1) * CH].astype(f32).astype(bf16)
+        annot[c, 0:128, :] = a
+        annot[c, 128:144, :] = tail
+        count = count + lax.dot_general(
+            jnp.ones((8, CH), bf16), a, (((1,), (1,)), ((), ())), preferred_element_type=f32
+        )
+    cnt[0] = count
+    acc[...] = jnp.zeros_like(acc)
+    pl.semaphore_wait(barrier, 7 + groups - 1 + 3)
+
+    def remote(src, dst, s, r, wide, narrow):
+        return pltpu.make_async_remote_copy(
+            src_ref=src, dst_ref=dst, send_sem=s, recv_sem=r,
+            device_id=device(wide, narrow), device_id_type=MESH,
+        )
+
+    def count1(d):
+        return remote(
+            cnt.at[0], cnt_got.at[0, d], csend.at[0, d], crecv.at[0, d],
+            w - g + lax.rem(g + d, 8), n,
+        )
+
+    def count2(d):
+        return remote(
+            cnt.at[1], cnt_got.at[1, d], csend.at[1, d], crecv.at[1, d],
+            lax.rem(h + d, groups) * 8 + g, n,
+        )
+
+    for d in range(1, 8):
+        count1(d).start()
+
+    eps = 1e-05
+
+    def standardize(c):
+        def total(i, s):
+            x = geno[c, pl.ds(pl.multiple_of(i * 128, 128), 128), :].astype(f32)
+            return s + jnp.sum(x.reshape(16, 8, CH), axis=0)
+
+        def spread(i, s):
+            x = geno[c, pl.ds(pl.multiple_of(i * 128, 128), 128), :].astype(f32) - mean
+            return s + jnp.sum((x * x).reshape(16, 8, CH), axis=0)
+
+        zero = jnp.zeros((8, CH), f32)
+        blocks = samples // 128
+        mean = jnp.sum(lax.fori_loop(0, blocks, total, zero), axis=0, keepdims=True) / samples
+        var = jnp.sum(lax.fori_loop(0, blocks, spread, zero), axis=0, keepdims=True) / samples
+        inv = 1.0 / jnp.sqrt(var + eps)
+
+        def put(i, _):
+            at = pl.ds(pl.multiple_of(i * 128, 128), 128)
+            y = ((geno[c, at, :].astype(f32) - mean) * inv).astype(bf16)
+            geno[c, at, :] = y
+            genot[c, :, at] = y.T
+            return 0
+
+        lax.fori_loop(0, blocks, put, 0)
+
+    def halo_geno():
+        return remote(
+            geno.at[ob + csl], geno.at[12], send.at[0], recv.at[0], over, p
+        )
+
+    def halo_annot():
+        return remote(
+            annot.at[ob + csl], annot.at[12], send.at[1], recv.at[1], over, p
+        )
+
+    def mate_geno(q):
+        return remote(
+            geno.at[mb + q], geno.at[8 + q], send.at[2 + q], recv.at[2 + q], mate, n
+        )
+
+    def mate_annot():
+        return remote(
+            annot.at[pl.ds(mb, 4)], annot.at[pl.ds(8, 4)], send.at[6], recv.at[6], mate, n
+        )
+
+    halo_annot().start()
+    mate_annot().start()
+    load(0).wait()
+    standardize(ob + csl)
+    halo_geno().start()
+    for q in range(4):
+        load(1 + q).wait()
+
+    def mate_step(q, _):
+        standardize(mb + q)
+        mate_geno(q).start()
+        return 0
+
+    lax.fori_loop(0, 4, mate_step, 0)
+    for t in range(5, 8):
+        load(t).wait()
+
+    def rest_step(t, _):
+        standardize(ob + lax.rem(csl + t, 4))
+        return 0
+
+    lax.fori_loop(1, 4, rest_step, 0)
+
+    total_count = cnt[0]
+    for d in range(1, 8):
+        count1(d).wait_recv()
+        total_count = total_count + cnt_got[0, d]
+    cnt[1] = total_count
+    for d in range(1, groups):
+        count2(d).start()
+
+    k1 = (1.0 + 1.0 / (samples - 2)) / (float(samples) * samples)
+    k2 = 1.0 / (samples - 2)
+    diff = (
+        lax.broadcasted_iota(jnp.int32, (CH, CH), 0) - lax.broadcasted_iota(jnp.int32, (CH, CH), 1)
+    ).astype(f32)
+
+    def run(tiles, tile):
+        def weigh(t):
+            own, other, _, sign, limit, factor = tile(t)
+            products = jnp.dot(genot[own], geno[other], preferred_element_type=f32)
+            value = (products * products) * (k1 * factor) - k2 * factor
+            wbuf[lax.rem(t, 2)] = jnp.where(diff * sign <= limit, value, 0.0).astype(bf16)
+
+        def apply(t):
+            own, other, own_sum, _, _, _ = tile(t)
+            weights = wbuf[lax.rem(t, 2)]
+            acc[other] += jnp.dot(annot[own], weights, preferred_element_type=f32)
+            acc[own_sum] += lax.dot_general(
+                annot[other], weights, (((1,), (1,)), ((), ())), preferred_element_type=f32
+            )
+
+        weigh(jnp.int32(0))
+
+        def step(t, _):
+            apply(t - 1)
+            weigh(t)
+            return 0
+
+        lax.fori_loop(1, tiles, step, 0)
+        apply(jnp.int32(tiles - 1))
+
+    def at_least(t, bound):
+        return (t >= bound).astype(jnp.int32)
+
+    def local_tile(t):
+        off = at_least(t, 8) + at_least(t, 15) + at_least(t, 21) + at_least(t, 26)
+        base = 8 * at_least(t, 8) + 7 * at_least(t, 15) + 6 * at_least(t, 21) + 5 * at_least(t, 26)
+        low = t - base
+        high = low + off
+        return (
+            high, low, high, 1.0,
+            jnp.where(off == 4, 0.0, FAR), jnp.where(off == 0, 0.5, 1.0),
+        )
+
+    run(30, local_tile)
+
+    total_count = cnt[1]
+    for d in range(1, groups):
+        count2(d).wait_recv()
+        total_count = total_count + cnt_got[1, d]
+
+    mate_annot().wait_recv()
+    for q in range(4):
+        mate_geno(q).wait_recv()
+
+    def mate_tile(t):
+        u = at_least(t, 1) + at_least(t, 3) + at_least(t, 6)
+        v = t - at_least(t, 1) - 2 * at_least(t, 3) - 3 * at_least(t, 6)
+        own = mb + jnp.where(core == 0, u, v)
+        other = 8 + jnp.where(core == 0, v, u)
+        return (
+            own, other, own, jnp.where(core == 0, -1.0, 1.0),
+            jnp.where(u == v, 0.0, FAR), 1.0,
+        )
+
+    run(10, mate_tile)
+
+    halo_annot().wait_recv()
+    halo_geno().wait_recv()
+    open_end = jnp.where(core == 0, w == 0, w == wides - 1)
+
+    def halo_tile(t):
+        far = jnp.where(
+            core == 1, 256 * (t - n), jnp.where(t >= 2, 512 + 256 * (n - t), -4096)
+        )
+        limit = jnp.where(open_end, -4096, far).astype(f32)
+        return ob + t, jnp.int32(12), 13 + t, jnp.where(core == 0, 1.0, -1.0), limit, 1.0
+
+    run(4, halo_tile)
+
+    ri = lax.broadcasted_iota(jnp.int32, (128, 128), 0)
+    ci = lax.broadcasted_iota(jnp.int32, (128, 128), 1)
+    counts = jnp.sum(
+        jnp.where(ri == ci, jnp.broadcast_to(total_count[0:1, :], (128, 128)), 0.0),
+        axis=1, keepdims=True,
+    )
+    shares = counts / total_variants
+    zero_value = (0.0 - shares).astype(bf16).astype(f32)
+    step_value = (1.0 - shares).astype(bf16).astype(f32) - zero_value
+
+    def centred(c):
+        return zero_value * acc[c, 128:129, :] + step_value * acc[c, 0:128, :]
+
+    def halo_back(m):
+        return remote(
+            halo_out, halo_got.at[n], send.at[7 + m], recv.at[7 + n], over, m
+        )
+
+    def halo_back_from(m):
+        return remote(
+            halo_out, halo_got.at[m], send.at[7 + m], recv.at[7 + m], over, m
+        )
+
+    def twin(part):
+        return remote(
+            twin_out.at[pl.ds(2 * part, 2)], twin_got.at[pl.ds(2 * part, 2)],
+            send.at[9 + part], recv.at[9 + part], w, 1 - n,
+        )
+
+    halo_out[...] = centred(12)
+    for m in range(2):
+        halo_back(m).start()
+    for q in range(4):
+        twin_out[q] = centred(13 + q).astype(bf16)
+    twin(1).start()
+
+    @pl.when(core == 1)
+    def _():
+        twin(0).start()
+
+    @pl.when(core == 0)
+    def _():
+        twin_got[0:2] = jnp.zeros((2, 128, CH), bf16)
+
+    def columns(c):
+        return pl.ds(pl.multiple_of(c * CH, CH), CH)
+
+    for q in range(4):
+        out_ref[:, columns(mb + q)] = centred(mb + q)
+        out_ref[:, columns(ob + q)] = centred(ob + q) + centred(13 + q)
+    for m in range(2):
+        halo_back_from(m).wait_recv()
+        out_ref[:, columns(ob + 2 * core + m)] += halo_got[m]
+    twin(1).wait_recv()
+
+    @pl.when(core == 1)
+    def _():
+        twin(0).wait_recv()
+
+    for q in range(4):
+        out_ref[:, columns(ob + q)] += twin_got[q].astype(f32)
+
+    for d in range(1, 8):
+        count1(d).wait_send()
+    for d in range(1, groups):
+        count2(d).wait_send()
+    halo_geno().wait_send()
+    halo_annot().wait_send()
+    mate_annot().wait_send()
+    for q in range(4):
+        mate_geno(q).wait_send()
+    for m in range(2):
+        halo_back(m).wait_send()
+    twin(1).wait_send()
+
+    @pl.when(core == 1)
+    def _():
+        twin(0).wait_send()
+
+
+def strip_scores(dosage, annotations, total_variants):
+    f32 = jnp.float32
+    bf16 = jnp.bfloat16
+    samples = dosage.shape[0]
+    dma = pltpu.SemaphoreType.DMA
+    return pl.pallas_call(
+        functools.partial(scores_kernel, total_variants),
+        out_shape=jax.ShapeDtypeStruct((128, 8 * CH), f32),
+        in_specs=[pl.BlockSpec(memory_space=pl.ANY), pl.BlockSpec(memory_space=pltpu.VMEM)],
+        out_specs=pl.BlockSpec(memory_space=pltpu.VMEM),
+        scratch_shapes=[
+            pltpu.VMEM((13, samples, CH), bf16),
+            pltpu.VMEM((8, CH, samples), bf16),
+            pltpu.VMEM((13, ROWS, CH), bf16),
+            pltpu.VMEM((17, ROWS, CH), f32),
+            pltpu.VMEM((2, CH, CH), bf16),
+            pltpu.VMEM((2, 8, 128), f32),
+            pltpu.VMEM((2, 8, 8, 128), f32),
+            pltpu.VMEM((4, 128, CH), bf16),
+            pltpu.VMEM((4, 128, CH), bf16),
+            pltpu.VMEM((128, CH), f32),
+            pltpu.VMEM((2, 128, CH), f32),
+            dma((8,)), dma((11,)), dma((11,)), dma((2, 8)), dma((2, 8)),
+        ],
+        compiler_params=pltpu.CompilerParams(
+            collective_id=0, has_side_effects=True, vmem_limit_bytes=56 * 1024 * 1024
+        ),
+        name="scores",
+    )(dosage, annotations)
 
 
 TILES = 64
@@ -259,42 +586,10 @@
 
 
 def shards(dosage, annotations, test_statistic_table):
-    samples = dosage.shape[0]
-    strip_cols = dosage.shape[1]
-    half_width = strip_cols // 2
-    total_variants = lax.axis_size("wide") * strip_cols
-    wide_index = lax.axis_index("wide")
-    narrow_index = lax.axis_index("narrow")
-    values = dosage.astype(jnp.float32)
-    average = jnp.mean(values, axis=0)
-    centred_values = values - average[None, :]
-    variance = jnp.mean(centred_values * centred_values, axis=0)
-    standard = (centred_values / jnp.sqrt(variance + 1e-05)[None, :]).astype(jnp.bfloat16)
-    counts = lax.psum(jnp.sum(annotations.astype(jnp.float32), axis=1), "wide")
-    shares = counts / total_variants
-    centred = (annotations.astype(jnp.float32) - shares[:, None]).astype(jnp.bfloat16)
-    stacked = jnp.concatenate([standard, centred], axis=0)
-    row_local = narrow_index * half_width
-    strip_start = wide_index * strip_cols
-    row_start = strip_start + row_local
-    own_rows = lax.dynamic_slice_in_dim(standard, row_local, half_width, 1)
-    extended = extended_2(stacked, (("wide", 1),), half_width)
-    scores = jnp.zeros((centred.shape[0], half_width), jnp.float32)
-    for offset in range(3):
-        col_block = lax.dynamic_slice_in_dim(
-            extended, row_local + offset * half_width, half_width, 1
-        )
-        weights = band_weights(
-            col_block[:samples],
-            own_rows,
-            row_start - half_width + offset * half_width,
-            row_start,
-            total_variants,
-        )
-        scores = scores + jnp.dot(col_block[samples:], weights, preferred_element_type=jnp.float32)
-    strip_scores = lax.all_gather(scores, "narrow", axis=1, tiled=True)
-    totals = stats(strip_scores, test_statistic_table)
-    return finish(totals, strip_scores, test_statistic_table.shape[1], total_variants)
+    total_variants = lax.axis_size("wide") * dosage.shape[1]
+    scores = strip_scores(dosage, annotations, total_variants)
+    totals = stats(scores, test_statistic_table)
+    return finish(totals, scores, test_statistic_table.shape[1], total_variants)
 
 
 def solution(mesh):

time: 403 us -> 97.9 us (0.24)
  blocking collectives: 141 us -> 0 us
  waiting for transfers between devices: 113 us -> 0 us
  Pallas kernels: 38.3 us -> 95.9 us
  other arithmetic: 52.9 us -> 0 us
  matrix products: 31.6 us -> 0 us
  between operations: 14.1 us -> 0.67 us
  starting transfers between devices: 9.96 us -> 0 us
    psum x1 -> x0, blocking collectives: 141 us -> none  [shards(): counts = lax.psum(jnp.sum(annotations.astype(jnp.float32), axis=1), 'wide')]
    ppermute x2 -> x0, waiting for transfers between devices: 89.7 us -> none  [the longest x1 89.7 us: extended_2(): lax.ppermute(head, axis, [((i + 1) % count, i) for i in range(ends)])]
    pallas_call x0 -> x1, Pallas kernels: none -> 60.4 us  [strip_scores(): pl.pallas_call(functools.partial(scores_kernel, total_variants), out_shap...]
    concatenate x2 -> x0, other arithmetic: 35.4 us -> none  [the longest x1 23 us: extended_2(): jnp.concatenate([lax.ppermute(tail, axis, [(i, (i + 1) % count) for i in...]
    dot_general x3 -> x0, matrix products: 31.6 us -> none  [shards(): jnp.dot(col_block[samples:], weights, preferred_element_type=jnp.float32)]
    all_gather x1 -> x0, waiting for transfers between devices: 23.5 us -> none  [shards(): strip_scores = lax.all_gather(scores, 'narrow', axis=1, tiled=True)]
    convert_element_type x2 -> x0, other arithmetic: 10.2 us -> none  [the longest x1 10 us: shards(): (centred_values / jnp.sqrt(variance + 1e-05)[None, :]).astype(jnp.bfloat16)]
    ppermute x2 -> x0, starting transfers between devices: 9.92 us -> none  [the longest x1 7.82 us: extended_2(): lax.ppermute(head, axis, [((i + 1) % count, i) for i in range(ends)])]
  transfers between devices with their start and end apart: 3 -> 0, of which waited for: 2 -> 0; matrix products, arithmetic and copies ran while one was open for 0% -> 0% of each run, Pallas kernels for 0% -> 0%
where the time goes in v2:
time: 97.9 us; the launch traced here: 97.7 us
  Pallas kernels  95.9 us (98%)
  local copies, waits for them, and re-layouts  1.22 us (1%)
    pallas_call x1, Pallas kernels, strip_scores(): pl.pallas_call(functools.partial(scores_kernel, total_variants), out_shap...  60.4 us
    pallas_call x1, Pallas kernels, stats(): pl.pallas_call(stats_kernel, out_shape=jax.ShapeDtypeStruct((TILES * 8, 1...  20.7 us
    pallas_call x1, Pallas kernels, finish(): pl.pallas_call(functools.partial(finish_kernel, total_variants), out_shap...  14.7 us

profile of v2, /device:TPU:1, one launch (start us, length us, event | category | flops | bytes accessed | tf_op | source)
XLA Modules:
  0.0 97.7 jit_solution(2568140494376822758)
XLA Ops:
  0.6 0.0 copy-start.1
  0.6 60.4 %scores.1.s_ref = f32[128,2048]{1,0:T(8,128)} custom-call(bf16[2048,2048]{1,0:T(8,128)(2,1)} %x_ref.1, s32[128,2048]{1,0:T(8,128)} %ann_ref.1), custom_call_target="tpu_custom_call" | custom-call | tf_op jit(solution)/shard_map/scores/pallas_call | solution.py:362
  61.0 0.0 copy-done.1
  61.1 0.0 copy-start
  61.1 1.2 %copy-done = f32[128,2048]{1,0:T(8,128)S(1)} copy-done((f32[128,2048]{1,0:T(8,128)S(1)}, f32[128,2048]{1,0:T(8,128)}, u32[]{:S(2)}) %copy-start) | copy-done | bytes 1048600
  62.3 20.7 %stats.1.p_ref = f32[512,128]{1,0:T(8,128)S(1)} custom-call(f32[128,2048]{1,0:T(8,128)S(1)} %copy-done, f32[2048,256]{1,0:T(8,128)S(1)} %copy-done.1), custom_call_target="tpu_custom_call" | custom-call | tf_op jit(solution)/shard_map/stats/pallas_call | solution.py:505
  83.0 14.7 %finish.1 = (f32[128,1024]{1,0:T(8,128)}, f32[2048,256]{1,0:T(8,128)}) custom-call(f32[512,128]{1,0:T(8,128)S(1)} %stats.1.p_ref, f32[128,2048]{1,0:T(8,128)S(1)} %copy-done), custom_call_target="tpu_custom_call" | custom-call | tf_op jit(solution)/shard_map/finish/pallas_call | solution.py:575
Async XLA Ops:
  0.6 60.4 %copy-start.1 = (f32[2048,256]{1,0:T(8,128)S(1)}, f32[2048,256]{1,0:T(8,128)}, u32[]{:S(2)}) copy-start(f32[2048,256]{1,0:T(8,128)} %t_ref.1) | copy-start | bytes 6291460
  61.1 1.2 %copy-start = (f32[128,2048]{1,0:T(8,128)S(1)}, f32[128,2048]{1,0:T(8,128)}, u32[]{:S(2)}) copy-start(f32[128,2048]{1,0:T(8,128)} %scores.1.s_ref) | copy-start | bytes 3145732

commit v3 on v2

--- a/solution.py
+++ b/solution.py
@@ -26,12 +26,11 @@
 
 CH = 256
 ROWS = 144
-FAR = 4096.0
 
 
 def scores_kernel(
     total_variants, x_ref, ann_ref, out_ref,
-    geno, genot, annot, acc, wbuf, cnt, cnt_got, twin_out, twin_got, halo_out, halo_got,
+    geno, annot, acc, edge_acc, wbuf, edge, cnt, cnt_got, twin_out, twin_got, halo_out, halo_got,
     load_sem, send, recv, csend, crecv,
 ):
     f32 = jnp.float32
@@ -50,22 +49,28 @@
     left_chip = lax.rem(chip + core - 1 + wides // 2, wides // 2)
     turned = lax.rem(left_chip, 2)
     p = n + turned - 2 * n * turned
-    ob = core * 4
-    mb = 4 - ob
     csl = 2 * core + p
+    base = 4 * core
+    outer = 8 * core
+    beside = 8 - 8 * core
+
+    def columns(c, count=1):
+        return pl.ds(pl.multiple_of(c * CH, CH), count * CH)
+
+    def inner(i):
+        return jnp.where(core == 0, 3 - i, i)
 
     def device(wide, narrow):
         return {"wide": wide, "narrow": narrow}
 
-    def chunk_of(t):
-        rest = ob + lax.rem(csl + t + 4, 4)
-        return jnp.where(t == 0, ob + csl, jnp.where(t <= 4, mb + t - 1, rest))
-
     def load(t):
-        c = chunk_of(jnp.int32(t))
-        return pltpu.make_async_copy(
-            x_ref.at[:, pl.ds(pl.multiple_of(c * CH, CH), CH)], geno.at[c], load_sem.at[t]
-        )
+        if t == 0:
+            c = outer + csl
+        elif t <= 4:
+            c = 4 + inner(t - 1)
+        else:
+            c = outer + lax.rem(csl + t - 4, 4)
+        return pltpu.make_async_copy(x_ref.at[:, columns(c - base)], geno.at[:, columns(c)], load_sem.at[t])
 
     for t in range(8):
         load(t).start()
@@ -87,13 +92,17 @@
     count = jnp.zeros((8, 128), f32)
     for c in range(8):
         a = ann_ref[:, c * CH : (c + 1) * CH].astype(f32).astype(bf16)
-        annot[c, 0:128, :] = a
-        annot[c, 128:144, :] = tail
+        annot[0:128, columns(base + c)] = a
+        annot[128:144, columns(base + c)] = tail
         count = count + lax.dot_general(
             jnp.ones((8, CH), bf16), a, (((1,), (1,)), ((), ())), preferred_element_type=f32
         )
     cnt[0] = count
     acc[...] = jnp.zeros_like(acc)
+    ri = lax.broadcasted_iota(jnp.int32, (CH, CH), 0)
+    ci = lax.broadcasted_iota(jnp.int32, (CH, CH), 1)
+    edge[0] = jnp.where(core == 0, 0.5, jnp.where(ci <= ri, 1.0, 0.0))
+    edge[1] = jnp.where(core == 1, 0.5, jnp.where(ri <= ci, 1.0, 0.0))
     pl.semaphore_wait(barrier, 7 + groups - 1 + 3)
 
     def remote(src, dst, s, r, wide, narrow):
@@ -120,60 +129,74 @@
     eps = 1e-05
 
     def standardize(c):
-        def total(i, s):
-            x = geno[c, pl.ds(pl.multiple_of(i * 128, 128), 128), :].astype(f32)
-            return s + jnp.sum(x.reshape(16, 8, CH), axis=0)
-
-        def spread(i, s):
-            x = geno[c, pl.ds(pl.multiple_of(i * 128, 128), 128), :].astype(f32) - mean
-            return s + jnp.sum((x * x).reshape(16, 8, CH), axis=0)
+        at = columns(c)
+        block = 256
+
+        def rows(i):
+            return pl.ds(pl.multiple_of(i * block, block), block)
+
+        pivot = geno[0:16, at].astype(f32)[0:1]
+
+        def sums(i, s):
+            x = (geno[rows(i), at].astype(f32) - pivot).reshape(block // 8, 8, CH)
+            return s[0] + jnp.sum(x, axis=0), s[1] + jnp.sum(x * x, axis=0)
 
         zero = jnp.zeros((8, CH), f32)
-        blocks = samples // 128
-        mean = jnp.sum(lax.fori_loop(0, blocks, total, zero), axis=0, keepdims=True) / samples
-        var = jnp.sum(lax.fori_loop(0, blocks, spread, zero), axis=0, keepdims=True) / samples
-        inv = 1.0 / jnp.sqrt(var + eps)
+        first, second = lax.fori_loop(0, samples // block, sums, (zero, zero))
+        shift = jnp.sum(first, axis=0, keepdims=True) / samples
+        var = jnp.sum(second, axis=0, keepdims=True) / samples - shift * shift
+        mean = pivot + shift
+        inv = 1.0 / jnp.sqrt(jnp.maximum(var, 0.0) + eps)
 
         def put(i, _):
-            at = pl.ds(pl.multiple_of(i * 128, 128), 128)
-            y = ((geno[c, at, :].astype(f32) - mean) * inv).astype(bf16)
-            geno[c, at, :] = y
-            genot[c, :, at] = y.T
+            geno[rows(i), at] = ((geno[rows(i), at].astype(f32) - mean) * inv).astype(bf16)
             return 0
 
-        lax.fori_loop(0, blocks, put, 0)
+        lax.fori_loop(0, samples // block, put, 0)
 
     def halo_geno():
         return remote(
-            geno.at[ob + csl], geno.at[12], send.at[0], recv.at[0], over, p
+            geno.at[:, columns(outer + csl)], geno.at[:, columns(12)], send.at[0], recv.at[0], over, p
         )
 
     def halo_annot():
         return remote(
-            annot.at[ob + csl], annot.at[12], send.at[1], recv.at[1], over, p
+            annot.at[:, columns(outer + csl)], annot.at[:, columns(12)], send.at[1], recv.at[1], over, p
         )
 
     def mate_geno(q):
         return remote(
-            geno.at[mb + q], geno.at[8 + q], send.at[2 + q], recv.at[2 + q], mate, n
+            geno.at[:, columns(4 + q)], geno.at[:, columns(outer + q)],
+            send.at[2 + q], recv.at[2 + q], mate, n,
+        )
+
+    def mate_geno_from(q):
+        return remote(
+            geno.at[:, columns(4 + q)], geno.at[:, columns(beside + q)],
+            send.at[2 + q], recv.at[2 + q], mate, n,
         )
 
     def mate_annot():
         return remote(
-            annot.at[pl.ds(mb, 4)], annot.at[pl.ds(8, 4)], send.at[6], recv.at[6], mate, n
+            annot.at[:, columns(4, 4)], annot.at[:, columns(outer, 4)], send.at[6], recv.at[6], mate, n
+        )
+
+    def mate_annot_from():
+        return remote(
+            annot.at[:, columns(4, 4)], annot.at[:, columns(beside, 4)], send.at[6], recv.at[6], mate, n
         )
 
     halo_annot().start()
     mate_annot().start()
     load(0).wait()
-    standardize(ob + csl)
+    standardize(outer + csl)
     halo_geno().start()
     for q in range(4):
         load(1 + q).wait()
 
-    def mate_step(q, _):
-        standardize(mb + q)
-        mate_geno(q).start()
+    def mate_step(i, _):
+        standardize(4 + inner(i))
+        mate_geno(inner(i)).start()
         return 0
 
     lax.fori_loop(0, 4, mate_step, 0)
@@ -181,7 +204,7 @@
         load(t).wait()
 
     def rest_step(t, _):
-        standardize(ob + lax.rem(csl + t, 4))
+        standardize(outer + lax.rem(csl + t, 4))
         return 0
 
     lax.fori_loop(1, 4, rest_step, 0)
@@ -200,92 +223,84 @@
         lax.broadcasted_iota(jnp.int32, (CH, CH), 0) - lax.broadcasted_iota(jnp.int32, (CH, CH), 1)
     ).astype(f32)
 
-    def run(tiles, tile):
-        def weigh(t):
-            own, other, _, sign, limit, factor = tile(t)
-            products = jnp.dot(genot[own], geno[other], preferred_element_type=f32)
-            value = (products * products) * (k1 * factor) - k2 * factor
-            wbuf[lax.rem(t, 2)] = jnp.where(diff * sign <= limit, value, 0.0).astype(bf16)
-
-        def apply(t):
-            own, other, own_sum, _, _, _ = tile(t)
-            weights = wbuf[lax.rem(t, 2)]
-            acc[other] += jnp.dot(annot[own], weights, preferred_element_type=f32)
-            acc[own_sum] += lax.dot_general(
-                annot[other], weights, (((1,), (1,)), ((), ())), preferred_element_type=f32
-            )
-
-        weigh(jnp.int32(0))
-
-        def step(t, _):
-            apply(t - 1)
-            weigh(t)
-            return 0
-
-        lax.fori_loop(1, tiles, step, 0)
-        apply(jnp.int32(tiles - 1))
-
-    def at_least(t, bound):
-        return (t >= bound).astype(jnp.int32)
-
-    def local_tile(t):
-        off = at_least(t, 8) + at_least(t, 15) + at_least(t, 21) + at_least(t, 26)
-        base = 8 * at_least(t, 8) + 7 * at_least(t, 15) + 6 * at_least(t, 21) + 5 * at_least(t, 26)
-        low = t - base
-        high = low + off
-        return (
-            high, low, high, 1.0,
-            jnp.where(off == 4, 0.0, FAR), jnp.where(off == 0, 0.5, 1.0),
-        )
-
-    run(30, local_tile)
-
+    def correlate(own, other):
+        products = lax.dot_general(
+            geno[:, columns(own)], geno[:, columns(other)], (((0,), (0,)), ((), ())),
+            preferred_element_type=f32,
+        )
+        return (products * products) * k1 - k2
+
+    def place(t):
+        return jnp.where(core == 0, t, 7 - t), jnp.where(core == 0, t, 11 - t)
+
+    def weigh(t):
+        own, other = place(t)
+        for b in range(5):
+            value = correlate(own + b, other)
+            if b in (0, 4):
+                value = value * edge[b // 4]
+            wbuf[lax.rem(t, 2), b * CH : (b + 1) * CH, :] = value.astype(bf16)
+
+    def apply(t):
+        own, other = place(t)
+        weights = wbuf[lax.rem(t, 2)]
+        acc[:, columns(other)] += jnp.dot(
+            annot[:, columns(own, 5)], weights, preferred_element_type=f32
+        )
+        acc[:, columns(own, 5)] += lax.dot_general(
+            annot[:, columns(other)], weights, (((1,), (1,)), ((), ())), preferred_element_type=f32
+        )
+
+    def step(t, _):
+        apply(t - 1)
+        weigh(t)
+        return 0
+
+    def late_step(t, _):
+        mate_geno_from(jnp.where(core == 0, t - 4, 7 - t)).wait_recv()
+        return step(t, 0)
+
+    weigh(jnp.int32(0))
+    lax.fori_loop(1, 4, step, 0)
     total_count = cnt[1]
     for d in range(1, groups):
         count2(d).wait_recv()
         total_count = total_count + cnt_got[1, d]
-
-    mate_annot().wait_recv()
-    for q in range(4):
-        mate_geno(q).wait_recv()
-
-    def mate_tile(t):
-        u = at_least(t, 1) + at_least(t, 3) + at_least(t, 6)
-        v = t - at_least(t, 1) - 2 * at_least(t, 3) - 3 * at_least(t, 6)
-        own = mb + jnp.where(core == 0, u, v)
-        other = 8 + jnp.where(core == 0, v, u)
-        return (
-            own, other, own, jnp.where(core == 0, -1.0, 1.0),
-            jnp.where(u == v, 0.0, FAR), 1.0,
-        )
-
-    run(10, mate_tile)
+    mate_annot_from().wait_recv()
+    lax.fori_loop(4, 8, late_step, 0)
 
     halo_annot().wait_recv()
     halo_geno().wait_recv()
+    apply(jnp.int32(7))
     open_end = jnp.where(core == 0, w == 0, w == wides - 1)
-
-    def halo_tile(t):
-        far = jnp.where(
-            core == 1, 256 * (t - n), jnp.where(t >= 2, 512 + 256 * (n - t), -4096)
-        )
-        limit = jnp.where(open_end, -4096, far).astype(f32)
-        return ob + t, jnp.int32(12), 13 + t, jnp.where(core == 0, 1.0, -1.0), limit, 1.0
-
-    run(4, halo_tile)
-
-    ri = lax.broadcasted_iota(jnp.int32, (128, 128), 0)
-    ci = lax.broadcasted_iota(jnp.int32, (128, 128), 1)
+    near = jnp.where(open_end, 8192, jnp.where(core == 0, -8192, CH * n))
+    far = jnp.where(core == 0, 512 + CH * n, 8192)
+    first_row = jnp.where(core == 0, 512, 0)
+    for b in range(4):
+        row = ri + b * CH
+        diff = row - ci
+        inside = (diff >= near) & (diff <= far) & (row >= first_row)
+        value = jnp.where(inside, correlate(outer + b, 12), 0.0)
+        wbuf[0, b * CH : (b + 1) * CH, :] = value.astype(bf16)
+    weights = wbuf[0, 0 : 4 * CH, :]
+    acc[:, columns(12)] = jnp.dot(
+        annot[:, columns(outer, 4)], weights, preferred_element_type=f32
+    )
+    edge_acc[...] = lax.dot_general(
+        annot[:, columns(12)], weights, (((1,), (1,)), ((), ())), preferred_element_type=f32
+    )
+
+    eye = ri[:128, :128] == ci[:128, :128]
     counts = jnp.sum(
-        jnp.where(ri == ci, jnp.broadcast_to(total_count[0:1, :], (128, 128)), 0.0),
+        jnp.where(eye, jnp.broadcast_to(total_count[0:1, :], (128, 128)), 0.0),
         axis=1, keepdims=True,
     )
     shares = counts / total_variants
     zero_value = (0.0 - shares).astype(bf16).astype(f32)
     step_value = (1.0 - shares).astype(bf16).astype(f32) - zero_value
 
-    def centred(c):
-        return zero_value * acc[c, 128:129, :] + step_value * acc[c, 0:128, :]
+    def centred(sums):
+        return zero_value * sums[128:129, :] + step_value * sums[0:128, :]
 
     def halo_back(m):
         return remote(
@@ -303,11 +318,11 @@
             send.at[9 + part], recv.at[9 + part], w, 1 - n,
         )
 
-    halo_out[...] = centred(12)
+    halo_out[...] = centred(acc[:, columns(12)])
     for m in range(2):
         halo_back(m).start()
     for q in range(4):
-        twin_out[q] = centred(13 + q).astype(bf16)
+        twin_out[q] = centred(edge_acc[:, q * CH : (q + 1) * CH]).astype(bf16)
     twin(1).start()
 
     @pl.when(core == 1)
@@ -318,15 +333,17 @@
     def _():
         twin_got[0:2] = jnp.zeros((2, 128, CH), bf16)
 
-    def columns(c):
-        return pl.ds(pl.multiple_of(c * CH, CH), CH)
+    def out(c):
+        return columns(c - base)
 
     for q in range(4):
-        out_ref[:, columns(mb + q)] = centred(mb + q)
-        out_ref[:, columns(ob + q)] = centred(ob + q) + centred(13 + q)
+        out_ref[:, out(4 + q)] = centred(acc[:, columns(4 + q)])
+        out_ref[:, out(outer + q)] = centred(
+            acc[:, columns(outer + q)] + edge_acc[:, q * CH : (q + 1) * CH]
+        )
     for m in range(2):
         halo_back_from(m).wait_recv()
-        out_ref[:, columns(ob + 2 * core + m)] += halo_got[m]
+        out_ref[:, out(outer + 2 * core + m)] += halo_got[m]
     twin(1).wait_recv()
 
     @pl.when(core == 1)
@@ -334,7 +351,7 @@
         twin(0).wait_recv()
 
     for q in range(4):
-        out_ref[:, columns(ob + q)] += twin_got[q].astype(f32)
+        out_ref[:, out(outer + q)] += twin_got[q].astype(f32)
 
     for d in range(1, 8):
         count1(d).wait_send()
@@ -365,11 +382,12 @@
         in_specs=[pl.BlockSpec(memory_space=pl.ANY), pl.BlockSpec(memory_space=pltpu.VMEM)],
         out_specs=pl.BlockSpec(memory_space=pltpu.VMEM),
         scratch_shapes=[
-            pltpu.VMEM((13, samples, CH), bf16),
-            pltpu.VMEM((8, CH, samples), bf16),
-            pltpu.VMEM((13, ROWS, CH), bf16),
-            pltpu.VMEM((17, ROWS, CH), f32),
-            pltpu.VMEM((2, CH, CH), bf16),
+            pltpu.VMEM((samples, 13 * CH), bf16),
+            pltpu.VMEM((ROWS, 13 * CH), bf16),
+            pltpu.VMEM((ROWS, 13 * CH), f32),
+            pltpu.VMEM((ROWS, 4 * CH), f32),
+            pltpu.VMEM((2, 5 * CH, CH), bf16),
+            pltpu.VMEM((2, CH, CH), f32),
             pltpu.VMEM((2, 8, 128), f32),
             pltpu.VMEM((2, 8, 8, 128), f32),
             pltpu.VMEM((4, 128, CH), bf16),
@@ -379,7 +397,7 @@
             dma((8,)), dma((11,)), dma((11,)), dma((2, 8)), dma((2, 8)),
         ],
         compiler_params=pltpu.CompilerParams(
-            collective_id=0, has_side_effects=True, vmem_limit_bytes=56 * 1024 * 1024
+            collective_id=0, has_side_effects=True, vmem_limit_bytes=57 * 1024 * 1024
         ),
         name="scores",
     )(dosage, annotations)
@@ -547,21 +565,26 @@
 
     def step(i, carry):
         a, b = carry
+        cols = [jnp.broadcast_to(a[:, r : r + 1], (128, 128)) for r in range(8)]
+        panel = [c[:8] for c in cols]
+        right = [a[:8], b[:8, :128], b[:8, 128:]]
         for r in range(8):
-            col = a[:, r : r + 1]
-            ra = a[r : r + 1, :]
-            rb = b[r : r + 1, :]
-            inv = 1.0 / a[r : r + 1, r : r + 1]
-            ra = ra * inv
-            rb = rb * inv
-            a2 = a - col * ra
-            b2 = b - col * rb
+            pivots = [jnp.broadcast_to(c[r : r + 1], (8, 128)) for c in panel]
+            inv = 1.0 / pivots[r]
+            factor = panel[r]
             here = sub == r
-            a = jnp.concatenate([jnp.where(here, ra, a2[:8]), a2[8:]], axis=0)
-            b = jnp.concatenate([jnp.where(here, rb, b2[:8]), b2[8:]], axis=0)
-        a = pltpu.roll(jnp.concatenate([a[8:], a[:8]], axis=0), 120, 1)
-        b = jnp.concatenate([b[8:], b[:8]], axis=0)
-        return a, b
+            for c in range(r + 1, 8):
+                row = pivots[c] * inv
+                panel[c] = jnp.where(here, row, panel[c] - factor * row)
+            for k in range(3):
+                row = jnp.broadcast_to(right[k][r : r + 1], (8, 128)) * inv
+                right[k] = jnp.where(here, row, right[k] - factor * row)
+        rest = [a[8:], b[8:, :128], b[8:, 128:]]
+        for r in range(8):
+            col = cols[r][8:]
+            rest = [x - col * y[r : r + 1] for x, y in zip(rest, right)]
+        a, b0, b1 = (jnp.concatenate([x, y], axis=0) for x, y in zip(rest, right))
+        return pltpu.roll(a, 120, 1), jnp.concatenate([b0, b1], axis=1)
 
     _, coef = lax.fori_loop(0, 16, step, (cov, proj))
     cs = split(coef)

time: 97.9 us -> 83.3 us (0.85)
  Pallas kernels: 95.9 us -> 81.3 us
    pallas_call x1, Pallas kernels: 60.4 us -> 45.1 us  [strip_scores(): pl.pallas_call(functools.partial(scores_kernel, total_variants), out_shap...]
    pallas_call x1, Pallas kernels: 20.7 us -> 27.7 us  [stats(): pl.pallas_call(stats_kernel, out_shape=jax.ShapeDtypeStruct((TILES * 8, 1...]
    pallas_call x1, Pallas kernels: 14.7 us -> 8.53 us  [finish(): pl.pallas_call(functools.partial(finish_kernel, total_variants), out_shap...]
where the time goes in v3:
time: 83.3 us; the launch traced here: 83.2 us
  Pallas kernels  81.3 us (98%)
  local copies, waits for them, and re-layouts  1.22 us (1%)
    pallas_call x1, Pallas kernels, strip_scores(): pl.pallas_call(functools.partial(scores_kernel, total_variants), out_shap...  45.1 us
    pallas_call x1, Pallas kernels, stats(): pl.pallas_call(stats_kernel, out_shape=jax.ShapeDtypeStruct((TILES * 8, 1...  27.7 us
    pallas_call x1, Pallas kernels, finish(): pl.pallas_call(functools.partial(finish_kernel, total_variants), out_shap...  8.53 us

profile of v3, /device:TPU:1, one launch (start us, length us, event | category | flops | bytes accessed | tf_op | source)
XLA Modules:
  0.0 83.2 jit_solution(973110574466860288)
XLA Ops:
  0.6 0.0 copy-start.1
  0.6 45.1 %scores.1.s_ref = f32[128,2048]{1,0:T(8,128)} custom-call(bf16[2048,2048]{1,0:T(8,128)(2,1)} %x_ref.1, s32[128,2048]{1,0:T(8,128)} %ann_ref.1), custom_call_target="tpu_custom_call" | custom-call | tf_op jit(solution)/shard_map/scores/pallas_call | solution.py:379
  45.7 0.0 copy-done.1
  45.7 0.0 copy-start
  45.8 1.2 %copy-done = f32[128,2048]{1,0:T(8,128)S(1)} copy-done((f32[128,2048]{1,0:T(8,128)S(1)}, f32[128,2048]{1,0:T(8,128)}, u32[]{:S(2)}) %copy-start) | copy-done | bytes 1048600
  47.0 27.7 %stats.1.p_ref = f32[512,128]{1,0:T(8,128)S(1)} custom-call(f32[128,2048]{1,0:T(8,128)S(1)} %copy-done, f32[2048,256]{1,0:T(8,128)S(1)} %copy-done.1), custom_call_target="tpu_custom_call" | custom-call | tf_op jit(solution)/shard_map/stats/pallas_call | solution.py:523
  74.7 8.5 %finish.1 = (f32[128,1024]{1,0:T(8,128)}, f32[2048,256]{1,0:T(8,128)}) custom-call(f32[512,128]{1,0:T(8,128)S(1)} %stats.1.p_ref, f32[128,2048]{1,0:T(8,128)S(1)} %copy-done), custom_call_target="tpu_custom_call" | custom-call | tf_op jit(solution)/shard_map/finish/pallas_call | solution.py:598
Async XLA Ops:
  0.6 45.1 %copy-start.1 = (f32[2048,256]{1,0:T(8,128)S(1)}, f32[2048,256]{1,0:T(8,128)}, u32[]{:S(2)}) copy-start(f32[2048,256]{1,0:T(8,128)} %t_ref.1) | copy-start | bytes 6291460
  45.7 1.2 %copy-start = (f32[128,2048]{1,0:T(8,128)S(1)}, f32[128,2048]{1,0:T(8,128)}, u32[]{:S(2)}) copy-start(f32[128,2048]{1,0:T(8,128)} %scores.1.s_ref) | copy-start | bytes 3145732

commit v4 on v3

--- a/solution.py
+++ b/solution.py
@@ -29,9 +29,10 @@
 
 
 def scores_kernel(
-    total_variants, x_ref, ann_ref, out_ref,
-    geno, annot, acc, edge_acc, wbuf, edge, cnt, cnt_got, twin_out, twin_got, halo_out, halo_got,
-    load_sem, send, recv, csend, crecv,
+    total_variants, x_ref, ann_hbm, t_ref, out_hbm, total_ref,
+    ann_ref, out_ref, geno, annot, acc, edge_acc, wbuf, edge, cnt, cnt_got, twin_out, twin_got, halo_out, halo_got,
+    table, table_hi, table_lo, part, got1, sum1, got2, sum2, got3,
+    load_sem, send, recv, csend, crecv, ssend, srecv,
 ):
     f32 = jnp.float32
     bf16 = jnp.bfloat16
@@ -72,8 +73,20 @@
             c = outer + lax.rem(csl + t - 4, 4)
         return pltpu.make_async_copy(x_ref.at[:, columns(c - base)], geno.at[:, columns(c)], load_sem.at[t])
 
-    for t in range(8):
+    def load_table():
+        return pltpu.make_async_copy(t_ref, table, load_sem.at[8])
+
+    def load_annotations():
+        return pltpu.make_async_copy(ann_hbm, ann_ref, load_sem.at[9])
+
+    def store_scores():
+        return pltpu.make_async_copy(out_ref, out_hbm, load_sem.at[10])
+
+    load(0).start()
+    load_annotations().start()
+    for t in range(1, 8):
         load(t).start()
+    load_table().start()
 
     barrier = pltpu.get_barrier_semaphore()
 
@@ -90,6 +103,7 @@
 
     tail = jnp.where(lax.broadcasted_iota(jnp.int32, (16, CH), 0) == 0, 1.0, 0.0).astype(bf16)
     count = jnp.zeros((8, 128), f32)
+    load_annotations().wait()
     for c in range(8):
         a = ann_ref[:, c * CH : (c + 1) * CH].astype(f32).astype(bf16)
         annot[0:128, columns(base + c)] = a
@@ -103,7 +117,6 @@
     ci = lax.broadcasted_iota(jnp.int32, (CH, CH), 1)
     edge[0] = jnp.where(core == 0, 0.5, jnp.where(ci <= ri, 1.0, 0.0))
     edge[1] = jnp.where(core == 1, 0.5, jnp.where(ri <= ci, 1.0, 0.0))
-    pl.semaphore_wait(barrier, 7 + groups - 1 + 3)
 
     def remote(src, dst, s, r, wide, narrow):
         return pltpu.make_async_remote_copy(
@@ -122,9 +135,6 @@
             cnt.at[1], cnt_got.at[1, d], csend.at[1, d], crecv.at[1, d],
             lax.rem(h + d, groups) * 8 + g, n,
         )
-
-    for d in range(1, 8):
-        count1(d).start()
 
     eps = 1e-05
 
@@ -186,11 +196,14 @@
             annot.at[:, columns(4, 4)], annot.at[:, columns(beside, 4)], send.at[6], recv.at[6], mate, n
         )
 
+    load(0).wait()
+    standardize(outer + csl)
+    pl.semaphore_wait(barrier, 7 + groups - 1 + 3)
+    halo_geno().start()
     halo_annot().start()
     mate_annot().start()
-    load(0).wait()
-    standardize(outer + csl)
-    halo_geno().start()
+    for d in range(1, 8):
+        count1(d).start()
     for q in range(4):
         load(1 + q).wait()
 
@@ -208,6 +221,9 @@
         return 0
 
     lax.fori_loop(1, 4, rest_step, 0)
+    load_table().wait()
+    table_hi[...], table_lo[...] = split(table[...])
+    table_sum = jnp.sum(table[...], axis=0, keepdims=True)
 
     total_count = cnt[0]
     for d in range(1, 8):
@@ -256,8 +272,11 @@
         weigh(t)
         return 0
 
+    def inner_late(t):
+        return jnp.where(core == 0, t - 4, 7 - t)
+
     def late_step(t, _):
-        mate_geno_from(jnp.where(core == 0, t - 4, 7 - t)).wait_recv()
+        mate_geno_from(inner_late(t)).wait_recv()
         return step(t, 0)
 
     weigh(jnp.int32(0))
@@ -266,12 +285,9 @@
     for d in range(1, groups):
         count2(d).wait_recv()
         total_count = total_count + cnt_got[1, d]
-    mate_annot_from().wait_recv()
-    lax.fori_loop(4, 8, late_step, 0)
-
     halo_annot().wait_recv()
     halo_geno().wait_recv()
-    apply(jnp.int32(7))
+    apply(jnp.int32(3))
     open_end = jnp.where(core == 0, w == 0, w == wides - 1)
     near = jnp.where(open_end, 8192, jnp.where(core == 0, -8192, CH * n))
     far = jnp.where(core == 0, 512 + CH * n, 8192)
@@ -318,7 +334,7 @@
             send.at[9 + part], recv.at[9 + part], w, 1 - n,
         )
 
-    halo_out[...] = centred(acc[:, columns(12)])
+    halo_out[...] = centred(acc[:, columns(12)]).astype(bf16)
     for m in range(2):
         halo_back(m).start()
     for q in range(4):
@@ -333,6 +349,12 @@
     def _():
         twin_got[0:2] = jnp.zeros((2, 128, CH), bf16)
 
+    mate_annot_from().wait_recv()
+    mate_geno_from(inner_late(4)).wait_recv()
+    weigh(jnp.int32(4))
+    lax.fori_loop(5, 8, late_step, 0)
+    apply(jnp.int32(7))
+
     def out(c):
         return columns(c - base)
 
@@ -343,7 +365,7 @@
         )
     for m in range(2):
         halo_back_from(m).wait_recv()
-        out_ref[:, out(outer + 2 * core + m)] += halo_got[m]
+        out_ref[:, out(outer + 2 * core + m)] += halo_got[m].astype(f32)
     twin(1).wait_recv()
 
     @pl.when(core == 1)
@@ -353,6 +375,103 @@
     for q in range(4):
         out_ref[:, out(outer + q)] += twin_got[q].astype(f32)
 
+    store_scores().start()
+    dg = functools.partial(lax.dot_general, preferred_element_type=f32)
+    scores = split(out_ref[...])
+    proj = dot3(scores, (table_hi[...], table_lo[...]), ((1,), (0,)))
+    part[96:224, :] = proj[:, :128]
+    part[224:352, :] = proj[:, 128:]
+    cross = dot3(scores, scores, ((1,), (1,)))
+    low = lax.broadcasted_iota(jnp.int32, (64, 128), 1) < 64
+    part[0:64, :] = jnp.where(low, cross[:64], cross[64:])
+    part[64:96, :] = jnp.where(low[:32], pltpu.roll(cross[0:32], 64, 1), cross[32:64])
+    ones = jnp.ones((8, 8 * CH), bf16)
+    by_lane = (((1,), (1,)), ((), ()))
+    score_sum = dg(ones, scores[0], by_lane) + dg(ones, scores[1], by_lane)
+    line = lax.broadcasted_iota(jnp.int32, (8, 128), 0)
+    sums = jnp.where(line == 0, score_sum, 0.0)
+    sums = jnp.where(line == 1, table_sum[:, :128], sums)
+    sums = jnp.where(line == 2, table_sum[:, 128:], sums)
+    part[352:360, :] = sums
+    part[360:384, :] = jnp.zeros((24, 128), f32)
+
+    def in_block(d):
+        return lax.rem(g + d, 8)
+
+    def across(d):
+        return lax.rem(h + d, groups)
+
+    def piece(i, size):
+        return pl.ds(pl.multiple_of(i * size, size), size)
+
+    def copy1(d):
+        return remote(
+            part.at[piece(in_block(d), 48)], got1.at[d - 1], ssend.at[0, d], srecv.at[0, d],
+            w - g + in_block(d), n,
+        )
+
+    def copy2(d):
+        return remote(
+            sum1.at[piece(across(d), 8)], got2.at[d - 1], ssend.at[1, d], srecv.at[1, d],
+            across(d) * 8 + g, n,
+        )
+
+    def copy3(d):
+        return remote(
+            sum2, got3.at[piece(h, 8)], ssend.at[2, d], srecv.at[2, d], across(d) * 8 + g, n
+        )
+
+    def copy3_from(d):
+        return remote(
+            sum2, got3.at[piece(lax.rem(h - d + groups, groups), 8)],
+            ssend.at[2, d], srecv.at[2, d], across(d) * 8 + g, n,
+        )
+
+    def copy4(d):
+        return remote(
+            got3.at[pl.ds(0, 48)], total_ref.at[piece(g, 48)], ssend.at[3, d], srecv.at[3, d],
+            w - g + in_block(d), n,
+        )
+
+    def copy4_from(d):
+        return remote(
+            got3.at[pl.ds(0, 48)], total_ref.at[piece(lax.rem(g - d + 8, 8), 48)],
+            ssend.at[3, d], srecv.at[3, d], w - g + in_block(d), n,
+        )
+
+    for d in range(1, 8):
+        copy1(d).start()
+    total = part[piece(g, 48), :]
+    for d in range(1, 8):
+        copy1(d).wait_recv()
+        total = total + got1[d - 1]
+    sum1[0:48, :] = total
+    sum1[48:64, :] = jnp.zeros((16, 128), f32)
+    for d in range(1, groups):
+        copy2(d).start()
+    total = sum1[piece(h, 8), :]
+    for d in range(1, groups):
+        copy2(d).wait_recv()
+        total = total + got2[d - 1]
+    sum2[...] = total
+    for d in range(1, groups):
+        copy3(d).start()
+    got3[piece(h, 8), :] = total
+    for d in range(1, groups):
+        copy3_from(d).wait_recv()
+    for d in range(1, 8):
+        copy4(d).start()
+    total_ref[piece(g, 48), :] = got3[0:48, :]
+    for d in range(1, 8):
+        copy4_from(d).wait_recv()
+    for d in range(1, 8):
+        copy1(d).wait_send()
+        copy4(d).wait_send()
+    for d in range(1, groups):
+        copy2(d).wait_send()
+        copy3(d).wait_send()
+
+    store_scores().wait()
     for d in range(1, 8):
         count1(d).wait_send()
     for d in range(1, groups):
@@ -371,17 +490,24 @@
         twin(0).wait_send()
 
 
-def strip_scores(dosage, annotations, total_variants):
+def strip_scores(dosage, annotations, table, total_variants):
     f32 = jnp.float32
     bf16 = jnp.bfloat16
     samples = dosage.shape[0]
     dma = pltpu.SemaphoreType.DMA
+    hbm = pl.BlockSpec(memory_space=pltpu.HBM)
+    vmem = pl.BlockSpec(memory_space=pltpu.VMEM)
     return pl.pallas_call(
         functools.partial(scores_kernel, total_variants),
-        out_shape=jax.ShapeDtypeStruct((128, 8 * CH), f32),
-        in_specs=[pl.BlockSpec(memory_space=pl.ANY), pl.BlockSpec(memory_space=pltpu.VMEM)],
-        out_specs=pl.BlockSpec(memory_space=pltpu.VMEM),
+        out_shape=(
+            jax.ShapeDtypeStruct((128, 8 * CH), f32),
+            jax.ShapeDtypeStruct((384, 128), f32),
+        ),
+        in_specs=[hbm, hbm, hbm],
+        out_specs=(hbm, vmem),
         scratch_shapes=[
+            pltpu.VMEM(annotations.shape, jnp.int32),
+            pltpu.VMEM((128, 8 * CH), f32),
             pltpu.VMEM((samples, 13 * CH), bf16),
             pltpu.VMEM((ROWS, 13 * CH), bf16),
             pltpu.VMEM((ROWS, 13 * CH), f32),
@@ -392,174 +518,49 @@
             pltpu.VMEM((2, 8, 8, 128), f32),
             pltpu.VMEM((4, 128, CH), bf16),
             pltpu.VMEM((4, 128, CH), bf16),
-            pltpu.VMEM((128, CH), f32),
-            pltpu.VMEM((2, 128, CH), f32),
-            dma((8,)), dma((11,)), dma((11,)), dma((2, 8)), dma((2, 8)),
-        ],
-        compiler_params=pltpu.CompilerParams(
-            collective_id=0, has_side_effects=True, vmem_limit_bytes=57 * 1024 * 1024
-        ),
-        name="scores",
-    )(dosage, annotations)
-
-
-TILES = 64
-
-
-def stats_kernel(s_ref, t_ref, out_ref, part, got1, sum1, got2, sum2, got3, send, recv):
-    w = lax.axis_index("wide")
-    g = lax.rem(w, 8)
-    h = lax.div(w, 8)
-
-    barrier = pltpu.get_barrier_semaphore()
-    for d in range(1, 8):
-        pl.semaphore_signal(
-            barrier, inc=1, device_id={"wide": w - g + lax.rem(g + d, 8)}, device_id_type=MESH
-        )
-        pl.semaphore_signal(
-            barrier, inc=1, device_id={"wide": lax.rem(h + d, 8) * 8 + g}, device_id_type=MESH
-        )
-
-    s = s_ref[...]
-    t = t_ref[...]
-    ss = split(s)
-    ts = split(t)
-    part[0:128, :] = dot3(ss, ss, ((1,), (1,)))
-    proj = dot3(ss, ts, ((1,), (0,)))
-    part[128:256, :] = proj[:, :128]
-    part[256:384, :] = proj[:, 128:]
-    ones = jnp.ones((8, s.shape[1]), jnp.bfloat16)
-    dg = functools.partial(lax.dot_general, preferred_element_type=jnp.float32)
-    ssum = dg(ones, ss[0], (((1,), (1,)), ((), ()))) + dg(ones, ss[1], (((1,), (1,)), ((), ())))
-    tsum = jnp.sum(t, axis=0, keepdims=True)
-    rows = lax.broadcasted_iota(jnp.int32, (8, 128), 0)
-    sums = jnp.where(rows == 0, ssum, 0.0)
-    sums = jnp.where(rows == 1, tsum[:, :128], sums)
-    sums = jnp.where(rows == 2, tsum[:, 128:], sums)
-    part[384:392, :] = sums
-    part[392:512, :] = jnp.zeros((120, 128), jnp.float32)
-
-    pl.semaphore_wait(barrier, 14)
-
-    def in_block(d):
-        return lax.rem(g + d, 8)
-
-    def across(d):
-        return lax.rem(h + d, 8)
-
-    def copy1(d):
-        p = in_block(d)
-        return pltpu.make_async_remote_copy(
-            src_ref=part.at[pl.ds(pl.multiple_of(p * 64, 64), 64)],
-            dst_ref=got1.at[d - 1],
-            send_sem=send.at[0, d],
-            recv_sem=recv.at[0, d],
-            device_id={"wide": w - g + p},
-            device_id_type=MESH,
-        )
-
-    def copy2(d):
-        p = across(d)
-        return pltpu.make_async_remote_copy(
-            src_ref=sum1.at[pl.ds(pl.multiple_of(p * 8, 8), 8)],
-            dst_ref=got2.at[d - 1],
-            send_sem=send.at[1, d],
-            recv_sem=recv.at[1, d],
-            device_id={"wide": p * 8 + g},
-            device_id_type=MESH,
-        )
-
-    def copy3(d):
-        return pltpu.make_async_remote_copy(
-            src_ref=sum2,
-            dst_ref=got3.at[pl.ds(pl.multiple_of(h * 8, 8), 8)],
-            send_sem=send.at[2, d],
-            recv_sem=recv.at[2, d],
-            device_id={"wide": across(d) * 8 + g},
-            device_id_type=MESH,
-        )
-
-    def copy4(d):
-        return pltpu.make_async_remote_copy(
-            src_ref=got3,
-            dst_ref=out_ref.at[pl.ds(pl.multiple_of(g * 64, 64), 64)],
-            send_sem=send.at[3, d],
-            recv_sem=recv.at[3, d],
-            device_id={"wide": w - g + in_block(d)},
-            device_id_type=MESH,
-        )
-
-    for d in range(1, 8):
-        copy1(d).start()
-    acc = part[pl.ds(pl.multiple_of(g * 64, 64), 64), :]
-    for d in range(1, 8):
-        copy1(d).wait_recv()
-        acc = acc + got1[d - 1]
-    sum1[...] = acc
-    for d in range(1, 8):
-        copy2(d).start()
-    acc = sum1[pl.ds(pl.multiple_of(h * 8, 8), 8), :]
-    for d in range(1, 8):
-        copy2(d).wait_recv()
-        acc = acc + got2[d - 1]
-    sum2[...] = acc
-    for d in range(1, 8):
-        copy3(d).start()
-    got3[pl.ds(pl.multiple_of(h * 8, 8), 8), :] = acc
-    for d in range(1, 8):
-        copy3(d).wait_recv()
-    for d in range(1, 8):
-        copy4(d).start()
-    out_ref[pl.ds(pl.multiple_of(g * 64, 64), 64), :] = got3[...]
-    for d in range(1, 8):
-        copy4(d).wait_recv()
-    for copy in (copy1, copy2, copy3, copy4):
-        for d in range(1, 8):
-            copy(d).wait_send()
-
-
-def stats(scores, table):
-    f32 = jnp.float32
-    return pl.pallas_call(
-        stats_kernel,
-        out_shape=jax.ShapeDtypeStruct((TILES * 8, 128), f32),
-        in_specs=[pl.BlockSpec(memory_space=pltpu.VMEM)] * 2,
-        out_specs=pl.BlockSpec(memory_space=pltpu.VMEM),
-        scratch_shapes=[
-            pltpu.VMEM((TILES * 8, 128), f32),
-            pltpu.VMEM((7, 64, 128), f32),
+            pltpu.VMEM((128, CH), bf16),
+            pltpu.VMEM((2, 128, CH), bf16),
+            pltpu.VMEM(table.shape, f32),
+            pltpu.VMEM(table.shape, bf16),
+            pltpu.VMEM(table.shape, bf16),
+            pltpu.VMEM((384, 128), f32),
+            pltpu.VMEM((7, 48, 128), f32),
             pltpu.VMEM((64, 128), f32),
             pltpu.VMEM((7, 8, 128), f32),
             pltpu.VMEM((8, 128), f32),
             pltpu.VMEM((64, 128), f32),
-            pltpu.SemaphoreType.DMA((4, 8)),
-            pltpu.SemaphoreType.DMA((4, 8)),
+            dma((11,)), dma((11,)), dma((11,)), dma((2, 8)), dma((2, 8)), dma((4, 8)), dma((4, 8)),
         ],
         compiler_params=pltpu.CompilerParams(
-            collective_id=1, has_side_effects=True, vmem_limit_bytes=32 * 1024 * 1024
+            collective_id=0, has_side_effects=True, vmem_limit_bytes=60 * 1024 * 1024
         ),
-        name="stats",
-    )(scores, table)
-
-
-def finish_kernel(total_variants, p_ref, s_ref, ld_ref, fit_ref):
+        name="scores",
+    )(dosage, annotations, table)
+
+
+def finish_kernel(total_variants, p_ref, s_hbm, ld_ref, fit_ref, s_ref, sem):
     n = lax.axis_index("narrow")
+    fetch = pltpu.make_async_copy(s_hbm, s_ref, sem)
+    fetch.start()
     scale = 1.0 / total_variants
-    sums = p_ref[384:392, :] * scale
+    sums = p_ref[352:360, :] * scale
     m_row = sums[0:1, :]
     chi = jnp.concatenate([sums[1:2, :], sums[2:3, :]], axis=1)
     ri = lax.broadcasted_iota(jnp.int32, (128, 128), 0)
     ci = lax.broadcasted_iota(jnp.int32, (128, 128), 1)
     eye = ri == ci
     m_col = jnp.sum(jnp.where(eye, jnp.broadcast_to(m_row, (128, 128)), 0.0), axis=1, keepdims=True)
-    cov = p_ref[0:128, :] * scale - m_col * m_row
-    proj = jnp.concatenate([p_ref[128:256, :], p_ref[256:384, :]], axis=1) * scale - m_col * chi
+    low = ci[:64] < 64
+    pair = p_ref[0:64, :]
+    above = p_ref[64:96, :]
+    above = jnp.concatenate([pltpu.roll(above, 64, 1), above], axis=0)
+    zeros = jnp.zeros((64, 128), jnp.float32)
+    above_only = jnp.concatenate([jnp.where(low, zeros, above), zeros], axis=0)
+    cross = jnp.concatenate([jnp.where(low, pair, above), jnp.where(low, zeros, pair)], axis=0)
+    cov = (cross + above_only.T) * scale - m_col * m_row
+    proj = jnp.concatenate([p_ref[96:224, :], p_ref[224:352, :]], axis=1) * scale - m_col * chi
     var = jnp.sum(jnp.where(eye, cov, 0.0), axis=1, keepdims=True)
     rstd = 1.0 / jnp.sqrt(var + 1e-05)
-
-    half = ld_ref.shape[1]
-    own = s_ref[:, pl.ds(pl.multiple_of(n * half, half), half)]
-    ld_ref[...] = (own - m_col) * rstd
 
     sub = lax.broadcasted_iota(jnp.int32, (8, 1), 0)
 
@@ -587,6 +588,10 @@
         return pltpu.roll(a, 120, 1), jnp.concatenate([b0, b1], axis=1)
 
     _, coef = lax.fori_loop(0, 16, step, (cov, proj))
+    fetch.wait()
+    half = ld_ref.shape[1]
+    own = s_ref[:, pl.ds(pl.multiple_of(n * half, half), half)]
+    ld_ref[...] = (own - m_col) * rstd
     cs = split(coef)
     rows = 256
     for k in range(fit_ref.shape[0] // rows):
@@ -601,17 +606,19 @@
             jax.ShapeDtypeStruct((128, scores.shape[1] // 2), jnp.float32),
             jax.ShapeDtypeStruct((scores.shape[1], traits), jnp.float32),
         ),
-        in_specs=[pl.BlockSpec(memory_space=pltpu.VMEM)] * 2,
+        in_specs=[
+            pl.BlockSpec(memory_space=pltpu.VMEM), pl.BlockSpec(memory_space=pltpu.HBM)
+        ],
         out_specs=(pl.BlockSpec(memory_space=pltpu.VMEM),) * 2,
-        compiler_params=pltpu.CompilerParams(vmem_limit_bytes=32 * 1024 * 1024),
+        scratch_shapes=[pltpu.VMEM(scores.shape, jnp.float32), pltpu.SemaphoreType.DMA],
+        compiler_params=pltpu.CompilerParams(vmem_limit_bytes=60 * 1024 * 1024),
         name="finish",
     )(totals, scores)
 
 
 def shards(dosage, annotations, test_statistic_table):
     total_variants = lax.axis_size("wide") * dosage.shape[1]
-    scores = strip_scores(dosage, annotations, total_variants)
-    totals = stats(scores, test_statistic_table)
+    scores, totals = strip_scores(dosage, annotations, test_statistic_table, total_variants)
     return finish(totals, scores, test_statistic_table.shape[1], total_variants)
 
 

time: 83.3 us -> 73.4 us (0.88)
  Pallas kernels: 81.3 us -> 72.5 us
  local copies, waits for them, and re-layouts: 1.22 us -> 0 us
    pallas_call x1 -> x0, Pallas kernels: 27.7 us -> none  [stats(): pl.pallas_call(stats_kernel, out_shape=jax.ShapeDtypeStruct((TILES * 8, 1...]
    pallas_call x1, Pallas kernels: 45.1 us -> 62.8 us  [strip_scores(): pl.pallas_call(functools.partial(scores_kernel, total_variants), out_shap...]
    unnamed x4 -> x0, local copies, waits for them, and re-layouts: 1.22 us -> none
    pallas_call x1, Pallas kernels: 8.53 us -> 9.68 us  [finish(): pl.pallas_call(functools.partial(finish_kernel, total_variants), out_shap...]
where the time goes in v4:
time: 73.4 us; the launch traced here: 73.3 us
  Pallas kernels  72.5 us (99%)
  between operations  0.8 us (1%)
    pallas_call x1, Pallas kernels, strip_scores(): pl.pallas_call(functools.partial(scores_kernel, total_variants), out_shap...  62.8 us
    pallas_call x1, Pallas kernels, finish(): pl.pallas_call(functools.partial(finish_kernel, total_variants), out_shap...  9.68 us

profile of v4, /device:TPU:1, one launch (start us, length us, event | category | flops | bytes accessed | tf_op | source)
XLA Modules:
  0.0 73.3 jit_solution(297427863193841758)
XLA Ops:
  0.6 62.8 %scores.1 = (f32[128,2048]{1,0:T(8,128)}, f32[384,128]{1,0:T(8,128)}) custom-call(bf16[2048,2048]{1,0:T(8,128)(2,1)} %x_ref.1, s32[128,2048]{1,0:T(8,128)} %ann_hbm.1, f32[2048,256]{1,0:T(8,128)} %t_ref.1), custom_call_target="tpu_custom_call" | custom-call | tf_op jit(solution)/shard_map/scores/pallas_call | solution.py:500
  63.4 9.7 %finish.1 = (f32[128,1024]{1,0:T(8,128)}, f32[2048,256]{1,0:T(8,128)}) custom-call(f32[384,128]{1,0:T(8,128)} %get-tuple-element.4.p_ref, f32[128,2048]{1,0:T(8,128)} %get-tuple-element.5.s_hbm), custom_call_target="tpu_custom_call" | custom-call | tf_op jit(solution)/shard_map/finish/pallas_call | solution.py:603

commit v5 on v4

--- a/solution.py
+++ b/solution.py
@@ -26,12 +26,13 @@
 
 CH = 256
 ROWS = 144
+PER_CORE = 23
 
 
 def scores_kernel(
     total_variants, x_ref, ann_hbm, t_ref, out_hbm, total_ref,
     ann_ref, out_ref, geno, annot, acc, edge_acc, wbuf, edge, cnt, cnt_got, twin_out, twin_got, halo_out, halo_got,
-    table, table_hi, table_lo, part, got1, sum1, got2, sum2, got3,
+    table, table_hi, table_lo, part, got_half, half_sum, got_tiles, tile_sum,
     load_sem, send, recv, csend, crecv, ssend, srecv,
 ):
     f32 = jnp.float32
@@ -45,6 +46,7 @@
     g = lax.rem(w, 8)
     h = lax.div(w, 8)
     groups = wides // 8
+    chips = wides // 2
     mate = w + 1 - 2 * core
     over = lax.rem(w + 2 * core - 1 + wides, wides)
     left_chip = lax.rem(chip + core - 1 + wides // 2, wides // 2)
@@ -88,6 +90,7 @@
         load(t).start()
     load_table().start()
 
+    twin_got[...] = jnp.zeros(twin_got.shape, bf16)
     barrier = pltpu.get_barrier_semaphore()
 
     def hello(wide, narrow):
@@ -95,8 +98,12 @@
 
     for d in range(1, 8):
         hello(w - g + lax.rem(g + d, 8), n)
-    for d in range(1, groups):
-        hello(lax.rem(h + d, groups) * 8 + g, n)
+
+    def hello_chip(d, _):
+        hello(lax.rem(w + 2 * d, wides), n)
+        return 0
+
+    lax.fori_loop(1, chips, hello_chip, 0)
     hello(w, 1 - n)
     hello(over, 0)
     hello(over, 1)
@@ -198,7 +205,7 @@
 
     load(0).wait()
     standardize(outer + csl)
-    pl.semaphore_wait(barrier, 7 + groups - 1 + 3)
+    pl.semaphore_wait(barrier, 7 + chips - 1 + 3)
     halo_geno().start()
     halo_annot().start()
     mate_annot().start()
@@ -281,6 +288,7 @@
 
     weigh(jnp.int32(0))
     lax.fori_loop(1, 4, step, 0)
+    mate_annot_from().wait_recv()
     total_count = cnt[1]
     for d in range(1, groups):
         count2(d).wait_recv()
@@ -328,28 +336,28 @@
             halo_out, halo_got.at[m], send.at[7 + m], recv.at[7 + m], over, m
         )
 
-    def twin(part):
-        return remote(
-            twin_out.at[pl.ds(2 * part, 2)], twin_got.at[pl.ds(2 * part, 2)],
-            send.at[9 + part], recv.at[9 + part], w, 1 - n,
-        )
+    def twin(q):
+        return remote(
+            twin_out.at[q], twin_got.at[q], send.at[9 + q], recv.at[9 + q], w, 1 - n
+        )
+
+    twin_sends = ((core == 1) & (n == 0), core == 1, None, (core == 1) | (n == 1))
+    twin_gets = ((core == 1) & (n == 1), core == 1, None, (core == 1) | (n == 0))
+
+    def where(conditions, q, act):
+        if conditions[q] is None:
+            act()
+        else:
+            pl.when(conditions[q])(act)
 
     halo_out[...] = centred(acc[:, columns(12)]).astype(bf16)
     for m in range(2):
         halo_back(m).start()
     for q in range(4):
         twin_out[q] = centred(edge_acc[:, q * CH : (q + 1) * CH]).astype(bf16)
-    twin(1).start()
-
-    @pl.when(core == 1)
-    def _():
-        twin(0).start()
-
-    @pl.when(core == 0)
-    def _():
-        twin_got[0:2] = jnp.zeros((2, 128, CH), bf16)
-
-    mate_annot_from().wait_recv()
+    for q in range(4):
+        where(twin_sends, q, twin(q).start)
+
     mate_geno_from(inner_late(4)).wait_recv()
     weigh(jnp.int32(4))
     lax.fori_loop(5, 8, late_step, 0)
@@ -366,12 +374,8 @@
     for m in range(2):
         halo_back_from(m).wait_recv()
         out_ref[:, out(outer + 2 * core + m)] += halo_got[m].astype(f32)
-    twin(1).wait_recv()
-
-    @pl.when(core == 1)
-    def _():
-        twin(0).wait_recv()
-
+    for q in range(4):
+        where(twin_gets, q, twin(q).wait_recv)
     for q in range(4):
         out_ref[:, out(outer + q)] += twin_got[q].astype(f32)
 
@@ -393,83 +397,76 @@
     sums = jnp.where(line == 1, table_sum[:, :128], sums)
     sums = jnp.where(line == 2, table_sum[:, 128:], sums)
     part[352:360, :] = sums
-    part[360:384, :] = jnp.zeros((24, 128), f32)
-
-    def in_block(d):
-        return lax.rem(g + d, 8)
-
-    def across(d):
-        return lax.rem(h + d, groups)
-
-    def piece(i, size):
-        return pl.ds(pl.multiple_of(i * size, size), size)
-
-    def copy1(d):
-        return remote(
-            part.at[piece(in_block(d), 48)], got1.at[d - 1], ssend.at[0, d], srecv.at[0, d],
-            w - g + in_block(d), n,
-        )
-
-    def copy2(d):
-        return remote(
-            sum1.at[piece(across(d), 8)], got2.at[d - 1], ssend.at[1, d], srecv.at[1, d],
-            across(d) * 8 + g, n,
-        )
-
-    def copy3(d):
-        return remote(
-            sum2, got3.at[piece(h, 8)], ssend.at[2, d], srecv.at[2, d], across(d) * 8 + g, n
-        )
-
-    def copy3_from(d):
-        return remote(
-            sum2, got3.at[piece(lax.rem(h - d + groups, groups), 8)],
-            ssend.at[2, d], srecv.at[2, d], across(d) * 8 + g, n,
-        )
-
-    def copy4(d):
-        return remote(
-            got3.at[pl.ds(0, 48)], total_ref.at[piece(g, 48)], ssend.at[3, d], srecv.at[3, d],
-            w - g + in_block(d), n,
-        )
-
-    def copy4_from(d):
-        return remote(
-            got3.at[pl.ds(0, 48)], total_ref.at[piece(lax.rem(g - d + 8, 8), 48)],
-            ssend.at[3, d], srecv.at[3, d], w - g + in_block(d), n,
-        )
-
-    for d in range(1, 8):
-        copy1(d).start()
-    total = part[piece(g, 48), :]
-    for d in range(1, 8):
-        copy1(d).wait_recv()
-        total = total + got1[d - 1]
-    sum1[0:48, :] = total
-    sum1[48:64, :] = jnp.zeros((16, 128), f32)
-    for d in range(1, groups):
-        copy2(d).start()
-    total = sum1[piece(h, 8), :]
-    for d in range(1, groups):
-        copy2(d).wait_recv()
-        total = total + got2[d - 1]
-    sum2[...] = total
-    for d in range(1, groups):
-        copy3(d).start()
-    got3[piece(h, 8), :] = total
-    for d in range(1, groups):
-        copy3_from(d).wait_recv()
-    for d in range(1, 8):
-        copy4(d).start()
-    total_ref[piece(g, 48), :] = got3[0:48, :]
-    for d in range(1, 8):
-        copy4_from(d).wait_recv()
-    for d in range(1, 8):
-        copy1(d).wait_send()
-        copy4(d).wait_send()
-    for d in range(1, groups):
-        copy2(d).wait_send()
-        copy3(d).wait_send()
+    part[360:368, :] = jnp.zeros((8, 128), f32)
+
+    half_rows = PER_CORE * 8
+
+    def tile(i):
+        return pl.ds(pl.multiple_of(i * 8, 8), 8)
+
+    def half_of(c):
+        return pl.ds(pl.multiple_of(c * half_rows, 8), half_rows)
+
+    swap = remote(part.at[half_of(1 - core)], got_half, ssend.at[0], srecv.at[0], mate, n)
+    swap.start()
+    swap.wait_recv()
+    half_sum[...] = part[half_of(core), :] + got_half[...]
+
+    def scatter(d, _):
+        q = lax.rem(chip + d, chips)
+
+        @pl.when(q < PER_CORE)
+        def _():
+            remote(
+                half_sum.at[tile(q)], got_tiles.at[d - 1], ssend.at[1], srecv.at[1], 2 * q + core, n
+            ).start()
+
+        return 0
+
+    lax.fori_loop(1, chips, scatter, 0)
+    mine = core * PER_CORE + chip
+    all_tiles = remote(got_tiles, got_tiles, ssend.at[1], srecv.at[1], mate, n)
+
+    def tiles(count, i):
+        ref = total_ref.at[pl.ds(0, count * 8)]
+        return remote(ref, ref, ssend.at[i], srecv.at[i], mate, n)
+
+    def for_others(act):
+        pl.when(chip < PER_CORE)(lambda: act(PER_CORE - 1))
+        pl.when(chip >= PER_CORE)(lambda: act(PER_CORE))
+
+    def hand_out(d, _):
+        q = lax.rem(chip + d, chips)
+        remote(
+            tile_sum, total_ref.at[tile(mine)], ssend.at[2], srecv.at[2], 2 * q + core, n
+        ).start()
+        return 0
+
+    @pl.when(chip < PER_CORE)
+    def _():
+        all_tiles.wait_recv()
+        total = half_sum[tile(chip), :] + jnp.sum(got_tiles[...], axis=0)
+        tile_sum[...] = total
+        lax.fori_loop(1, chips, hand_out, 0)
+        total_ref[tile(mine), :] = total
+
+    for_others(lambda count: tiles(count, 2).wait_recv())
+    exchange = remote(
+        total_ref.at[half_of(core)], total_ref.at[half_of(core)], ssend.at[3], srecv.at[3], mate, n
+    )
+    exchange_from = remote(
+        total_ref.at[half_of(1 - core)], total_ref.at[half_of(1 - core)], ssend.at[3], srecv.at[3],
+        mate, n,
+    )
+    exchange.start()
+    exchange_from.wait_recv()
+    swap.wait_send()
+    exchange.wait_send()
+    for_others(lambda count: tiles(count, 1).wait_send())
+
+    @pl.when(chip < PER_CORE)
+    def _():
+        remote(got_tiles, got_tiles, ssend.at[2], srecv.at[2], mate, n).wait_send()
 
     store_scores().wait()
     for d in range(1, 8):
@@ -483,11 +480,8 @@
         mate_geno(q).wait_send()
     for m in range(2):
         halo_back(m).wait_send()
-    twin(1).wait_send()
-
-    @pl.when(core == 1)
-    def _():
-        twin(0).wait_send()
+    for q in range(4):
+        where(twin_sends, q, twin(q).wait_send)
 
 
 def strip_scores(dosage, annotations, table, total_variants):
@@ -501,7 +495,7 @@
         functools.partial(scores_kernel, total_variants),
         out_shape=(
             jax.ShapeDtypeStruct((128, 8 * CH), f32),
-            jax.ShapeDtypeStruct((384, 128), f32),
+            jax.ShapeDtypeStruct((2 * PER_CORE * 8, 128), f32),
         ),
         in_specs=[hbm, hbm, hbm],
         out_specs=(hbm, vmem),
@@ -523,13 +517,12 @@
             pltpu.VMEM(table.shape, f32),
             pltpu.VMEM(table.shape, bf16),
             pltpu.VMEM(table.shape, bf16),
-            pltpu.VMEM((384, 128), f32),
-            pltpu.VMEM((7, 48, 128), f32),
-            pltpu.VMEM((64, 128), f32),
-            pltpu.VMEM((7, 8, 128), f32),
+            pltpu.VMEM((2 * PER_CORE * 8, 128), f32),
+            pltpu.VMEM((PER_CORE * 8, 128), f32),
+            pltpu.VMEM((PER_CORE * 8, 128), f32),
+            pltpu.VMEM((lax.axis_size("wide") // 2 - 1, 8, 128), f32),
             pltpu.VMEM((8, 128), f32),
-            pltpu.VMEM((64, 128), f32),
-            dma((11,)), dma((11,)), dma((11,)), dma((2, 8)), dma((2, 8)), dma((4, 8)), dma((4, 8)),
+            dma((11,)), dma((13,)), dma((13,)), dma((2, 8)), dma((2, 8)), dma((4,)), dma((4,)),
         ],
         compiler_params=pltpu.CompilerParams(
             collective_id=0, has_side_effects=True, vmem_limit_bytes=60 * 1024 * 1024

time: 73.4 us -> 69 us (0.940)
  Pallas kernels: 72.5 us -> 68.2 us
    pallas_call x1, Pallas kernels: 62.8 us -> 58.6 us  [strip_scores(): pl.pallas_call(functools.partial(scores_kernel, total_variants), out_shap...]
where the time goes in v5:
time: 69 us; the launch traced here: 68.9 us
  Pallas kernels  68.2 us (99%)
    pallas_call x1, Pallas kernels, strip_scores(): pl.pallas_call(functools.partial(scores_kernel, total_variants), out_shap...  58.6 us
    pallas_call x1, Pallas kernels, finish(): pl.pallas_call(functools.partial(finish_kernel, total_variants), out_shap...  9.69 us

profile of v5, /device:TPU:1, one launch (start us, length us, event | category | flops | bytes accessed | tf_op | source)
XLA Modules:
  0.0 68.9 jit_solution(3849043122461954885)
XLA Ops:
  0.6 58.6 %scores.1 = (f32[128,2048]{1,0:T(8,128)}, f32[368,128]{1,0:T(8,128)}) custom-call(bf16[2048,2048]{1,0:T(8,128)(2,1)} %x_ref.1, s32[128,2048]{1,0:T(8,128)} %ann_hbm.1, f32[2048,256]{1,0:T(8,128)} %t_ref.1), custom_call_target="tpu_custom_call" | custom-call | tf_op jit(solution)/shard_map/scores/pallas_call | solution.py:494
  59.2 9.7 %finish.1 = (f32[128,1024]{1,0:T(8,128)}, f32[2048,256]{1,0:T(8,128)}) custom-call(f32[368,128]{1,0:T(8,128)} %get-tuple-element.4.p_ref, f32[128,2048]{1,0:T(8,128)} %get-tuple-element.5.s_hbm), custom_call_target="tpu_custom_call" | custom-call | tf_op jit(solution)/shard_map/finish/pallas_call | solution.py:596

commit v6 on v5

--- a/solution.py
+++ b/solution.py
@@ -246,9 +246,9 @@
         lax.broadcasted_iota(jnp.int32, (CH, CH), 0) - lax.broadcasted_iota(jnp.int32, (CH, CH), 1)
     ).astype(f32)
 
-    def correlate(own, other):
+    def correlate(own, count, other):
         products = lax.dot_general(
-            geno[:, columns(own)], geno[:, columns(other)], (((0,), (0,)), ((), ())),
+            geno[:, columns(own, count)], geno[:, columns(other)], (((0,), (0,)), ((), ())),
             preferred_element_type=f32,
         )
         return (products * products) * k1 - k2
@@ -258,8 +258,9 @@
 
     def weigh(t):
         own, other = place(t)
+        values = correlate(own, 5, other)
         for b in range(5):
-            value = correlate(own + b, other)
+            value = values[b * CH : (b + 1) * CH]
             if b in (0, 4):
                 value = value * edge[b // 4]
             wbuf[lax.rem(t, 2), b * CH : (b + 1) * CH, :] = value.astype(bf16)
@@ -293,9 +294,9 @@
     for d in range(1, groups):
         count2(d).wait_recv()
         total_count = total_count + cnt_got[1, d]
+    apply(jnp.int32(3))
     halo_annot().wait_recv()
     halo_geno().wait_recv()
-    apply(jnp.int32(3))
     open_end = jnp.where(core == 0, w == 0, w == wides - 1)
     near = jnp.where(open_end, 8192, jnp.where(core == 0, -8192, CH * n))
     far = jnp.where(core == 0, 512 + CH * n, 8192)
@@ -304,7 +305,7 @@
         row = ri + b * CH
         diff = row - ci
         inside = (diff >= near) & (diff <= far) & (row >= first_row)
-        value = jnp.where(inside, correlate(outer + b, 12), 0.0)
+        value = jnp.where(inside, correlate(outer + b, 1, 12), 0.0)
         wbuf[0, b * CH : (b + 1) * CH, :] = value.astype(bf16)
     weights = wbuf[0, 0 : 4 * CH, :]
     acc[:, columns(12)] = jnp.dot(
@@ -557,11 +558,14 @@
 
     sub = lax.broadcasted_iota(jnp.int32, (8, 1), 0)
 
-    def step(i, carry):
-        a, b = carry
+    lane = lax.broadcasted_iota(jnp.int32, (8, 128), 1)
+    identity = jnp.where(lane == lax.broadcasted_iota(jnp.int32, (8, 128), 0), 1.0, 0.0)
+    first = lax.broadcasted_iota(jnp.int32, (120, 128), 1) < 8
+
+    def step(i, a):
         cols = [jnp.broadcast_to(a[:, r : r + 1], (128, 128)) for r in range(8)]
         panel = [c[:8] for c in cols]
-        right = [a[:8], b[:8, :128], b[:8, 128:]]
+        right = jnp.where(lane < 8, identity, a[:8])
         for r in range(8):
             pivots = [jnp.broadcast_to(c[r : r + 1], (8, 128)) for c in panel]
             inv = 1.0 / pivots[r]
@@ -570,17 +574,17 @@
             for c in range(r + 1, 8):
                 row = pivots[c] * inv
                 panel[c] = jnp.where(here, row, panel[c] - factor * row)
-            for k in range(3):
-                row = jnp.broadcast_to(right[k][r : r + 1], (8, 128)) * inv
-                right[k] = jnp.where(here, row, right[k] - factor * row)
-        rest = [a[8:], b[8:, :128], b[8:, 128:]]
+            row = jnp.broadcast_to(right[r : r + 1], (8, 128)) * inv
+            right = jnp.where(here, row, right - factor * row)
+        rest = jnp.where(first, 0.0, a[8:])
         for r in range(8):
-            col = cols[r][8:]
-            rest = [x - col * y[r : r + 1] for x, y in zip(rest, right)]
-        a, b0, b1 = (jnp.concatenate([x, y], axis=0) for x, y in zip(rest, right))
-        return pltpu.roll(a, 120, 1), jnp.concatenate([b0, b1], axis=1)
-
-    _, coef = lax.fori_loop(0, 16, step, (cov, proj))
+            rest = rest - cols[r][8:] * right[r : r + 1]
+        return pltpu.roll(jnp.concatenate([rest, right], axis=0), 120, 1)
+
+    inverse = lax.fori_loop(0, 16, step, cov, unroll=2)
+    coef = jnp.dot(
+        inverse, proj, precision=lax.Precision.HIGHEST, preferred_element_type=jnp.float32
+    )
     fetch.wait()
     half = ld_ref.shape[1]
     own = s_ref[:, pl.ds(pl.multiple_of(n * half, half), half)]

time: 69 us -> 68 us (0.986)
  Pallas kernels: 68.2 us -> 67.2 us
    pallas_call x1, Pallas kernels: 9.69 us -> 8.91 us  [finish(): pl.pallas_call(functools.partial(finish_kernel, total_variants), out_shap...]
where the time goes in v6:
time: 68 us; the launch traced here: 67.8 us
  Pallas kernels  67.2 us (99%)
    pallas_call x1, Pallas kernels, strip_scores(): pl.pallas_call(functools.partial(scores_kernel, total_variants), out_shap...  58.3 us
    pallas_call x1, Pallas kernels, finish(): pl.pallas_call(functools.partial(finish_kernel, total_variants), out_shap...  8.91 us

profile of v6, /device:TPU:1, one launch (start us, length us, event | category | flops | bytes accessed | tf_op | source)
XLA Modules:
  0.0 67.8 jit_solution(4007271063266743407)
XLA Ops:
  0.6 58.3 %scores.1 = (f32[128,2048]{1,0:T(8,128)}, f32[368,128]{1,0:T(8,128)}) custom-call(bf16[2048,2048]{1,0:T(8,128)(2,1)} %x_ref.1, s32[128,2048]{1,0:T(8,128)} %ann_hbm.1, f32[2048,256]{1,0:T(8,128)} %t_ref.1), custom_call_target="tpu_custom_call" | custom-call | tf_op jit(solution)/shard_map/scores/pallas_call | solution.py:495
  58.9 8.9 %finish.1 = (f32[128,1024]{1,0:T(8,128)}, f32[2048,256]{1,0:T(8,128)}) custom-call(f32[368,128]{1,0:T(8,128)} %get-tuple-element.4.p_ref, f32[128,2048]{1,0:T(8,128)} %get-tuple-element.5.s_hbm), custom_call_target="tpu_custom_call" | custom-call | tf_op jit(solution)/shard_map/finish/pallas_call | solution.py:600

commit v7 on v6

--- a/solution.py
+++ b/solution.py
@@ -147,7 +147,7 @@
 
     def standardize(c):
         at = columns(c)
-        block = 256
+        block = 512
 
         def rows(i):
             return pl.ds(pl.multiple_of(i * block, block), block)

time: 68 us -> 68.2 us (level)
  no operation moved by 1% of the time
where the time goes in v7:
time: 68.2 us; the launch traced here: 68.1 us
  Pallas kernels  67.3 us (99%)
  between operations  0.8 us (1%)
    pallas_call x1, Pallas kernels, strip_scores(): pl.pallas_call(functools.partial(scores_kernel, total_variants), out_shap...  58.4 us
    pallas_call x1, Pallas kernels, finish(): pl.pallas_call(functools.partial(finish_kernel, total_variants), out_shap...  8.91 us

profile of v7, /device:TPU:1, one launch (start us, length us, event | category | flops | bytes accessed | tf_op | source)
XLA Modules:
  0.0 68.1 jit_solution(7812531726077774990)
XLA Ops:
  0.6 58.4 %scores.1 = (f32[128,2048]{1,0:T(8,128)}, f32[368,128]{1,0:T(8,128)}) custom-call(bf16[2048,2048]{1,0:T(8,128)(2,1)} %x_ref.1, s32[128,2048]{1,0:T(8,128)} %ann_hbm.1, f32[2048,256]{1,0:T(8,128)} %t_ref.1), custom_call_target="tpu_custom_call" | custom-call | tf_op jit(solution)/shard_map/scores/pallas_call | solution.py:495
  59.0 8.9 %finish.1 = (f32[128,1024]{1,0:T(8,128)}, f32[2048,256]{1,0:T(8,128)}) custom-call(f32[368,128]{1,0:T(8,128)} %get-tuple-element.4.p_ref, f32[128,2048]{1,0:T(8,128)} %get-tuple-element.5.s_hbm), custom_call_target="tpu_custom_call" | custom-call | tf_op jit(solution)/shard_map/finish/pallas_call | solution.py:600
